TPU v7x, 32 devices: a whole 2x2x4 slice. The times are simulated.
32 devices in a mesh: row: 8 (over z, x), sub: 4 (over y, core).
Axes of the slice: x: 2, y: 2, z: 4, core: 2. Of those that a mesh axis runs over, the one named last changes fastest.
Arguments:
- feature_vectors: bfloat16 [2048, 1024], P('row'), may hold values from -6 to 6
- upstream_sensitivity: bfloat16 [2048, 1024], P('row'), may hold values from -0.4375 to 0.4375
- linear_mapping_matrix: bfloat16 [1024, 1024], P(None, 'sub'), may hold values from -0.1875 to 0.1875
- centroid_tables: float32 [128, 8, 256], P('sub'), may hold values from -6 to 6
- softness_factor: float32 [128], P('sub'), may hold values from 0.01 to 8
Outputs:
- input_grad: bfloat16 [2048, 1024], P('row', 'sub')
- rotation_grad: float32 [1024, 1024], P('row', 'sub')
- centroid_table_derivative: float32 [128, 8, 256], P('sub')
All inputs are finite; a program needn't handle non-finite values.
Results may differ from a plain program's by a relative error of at most 0.018.
Values may be sent and summed in bfloat16 or wider, within the bound.
A program may use at most 64 MiB of HBM per device.

v0:
```python
import functools

import jax
import jax.numpy as jnp
from jax import lax
from jax.experimental import pallas as pl
from jax.experimental.pallas import tpu as pltpu
from jax.sharding import PartitionSpec as P

MESH = pl.DeviceIdType.MESH
LOG2E = 1.4426950408889634
CHUNKS = 2
GROUP = 4
F32 = jnp.float32
BF16 = jnp.bfloat16


def nn(a, b):
    return lax.dot_general(a, b, (((1,), (0,)), ((), ())), preferred_element_type=F32)


def nt(a, b):
    return lax.dot_general(a, b, (((1,), (1,)), ((), ())), preferred_element_type=F32)


def low(x):
    return x.astype(BF16).astype(F32)


def split3(x):
    first = low(x)
    rest = x - first
    second = low(rest)
    return first, second, low(rest - second)


def split2(x):
    first = low(x)
    return first, low(x - first)


def for_peers(me, count, body):
    if count <= 8:
        for step in range(1, count):
            body(lax.rem(me + step, count))
    else:

        def run(step, carry):
            body(lax.rem(me + step, count))
            return carry

        lax.fori_loop(1, count, run, 0)


def subspaces(first, book_ref, temper_ref, turned_ref, slope_ref, grad_ref, recon_ref, cg_ref):
    width = 8
    codes = book_ref.shape[1]
    rows = turned_ref.shape[1]
    at = [pl.ds(pl.multiple_of((first + j) * width, width), width) for j in range(GROUP)]
    sub_k = lax.broadcasted_iota(jnp.int32, (width, codes), 0)
    sub_n = lax.broadcasted_iota(jnp.int32, (width, rows), 0)
    none_k = jnp.zeros((width, codes), F32)
    none_n = jnp.zeros((width, rows), F32)
    ones_n = jnp.where(sub_n < 3, 1.0, 0.0).astype(F32)
    one_k = jnp.where(sub_k == 0, 1.0, 0.0).astype(F32)
    both, books = [], []
    for j in range(GROUP):
        temper = temper_ref[first + j]
        c, z, g = book_ref[at[j], :], turned_ref[at[j], :], slope_ref[at[j], :]
        c1, c2, c3 = split3(c)
        square = jnp.sum(c * c, 0, keepdims=True) * (-LOG2E / jnp.full((1, codes), temper, F32))
        q1, q2, q3 = split3(square)
        squares = jnp.where(
            sub_k == 0, q1, jnp.where(sub_k == 1, q2, jnp.where(sub_k == 2, q3, 0.0))
        )
        left = jnp.concatenate([c1, c2, c3, c1, c2, c1, squares, none_k], 0).astype(BF16).T
        z1, z2, z3 = split3(z * (2.0 * LOG2E / jnp.full((1, rows), temper, F32)))
        g1, g2, g3 = split3(g)
        right = jnp.concatenate(
            [
                jnp.concatenate([z1, z1, z1, z2, z2, z3, ones_n, none_n], 0).astype(BF16),
                jnp.concatenate([g1, g1, g1, g2, g2, g3, none_n, none_n], 0).astype(BF16),
            ],
            1,
        )
        both.append(nn(left, right))
        books.append(jnp.concatenate([c1, c2, one_k, none_k], 0).astype(BF16))
    exps, exps_low = [], []
    for j in range(GROUP):
        s = both[j][:, :rows]
        e = jnp.exp2(s - jnp.max(s, 0, keepdims=True))
        exps.append(e)
        exps_low.append(e.astype(BF16))
    sums = [nn(books[j], exps_low[j]) for j in range(GROUP)]
    slopes, scales, backs = [], [], []
    for j in range(GROUP):
        back = 1.0 / sums[j][16:17]
        recon = (sums[j][0:8] + sums[j][8:16]) * back
        recon_ref[at[j], :] = recon
        mean = jnp.sum(slope_ref[at[j], :] * recon, 0, keepdims=True)
        slopes.append((exps[j] * (both[j][:, rows:] - mean)).astype(BF16))
        backs.append(back)
        scales.append(back * (2.0 / jnp.full((1, rows), temper_ref[first + j], F32)))
    for j in range(GROUP):
        c, z, g = book_ref[at[j], :], turned_ref[at[j], :], slope_ref[at[j], :]
        w = nn(books[j], slopes[j])
        total = w[16:17] * scales[j]
        grad_ref[at[j], :] = (w[0:8] + w[8:16]) * scales[j] - z * total
        a1, a2 = split2(g * backs[j])
        b1, b2 = split2(z * scales[j])
        t1, t2 = split2(scales[j])
        tops = jnp.where(sub_n == 0, t1, jnp.where(sub_n == 1, t2, 0.0))
        from_assign = nt(jnp.concatenate([a1, a2], 0).astype(BF16), exps_low[j])
        from_weight = nt(jnp.concatenate([b1, b2, tops, none_n], 0).astype(BF16), slopes[j])
        cg_ref[at[j], :] = (
            (from_assign[0:8] + from_assign[8:16])
            + (from_weight[0:8] + from_weight[8:16])
            - c * (from_weight[16:17] + from_weight[17:18])
        )


def kernel(
    row_count,
    sub_count,
    share_codes,
    x_ref,
    u_ref,
    w_ref,
    book_ref,
    temper_ref,
    input_ref,
    rotation_ref,
    codes_ref,
    xt,
    ut,
    turned,
    slope,
    grad,
    recon,
    cg,
    grad_low,
    in_out,
    in_got,
    rot_out,
    rot_got,
    cg_out,
    cg_got,
    cg_sum,
    cg_all,
    in_send,
    in_recv,
    rot_send,
    rot_recv,
    cg_send,
    cg_recv,
    all_send,
    all_recv,
):
    row, sub = lax.axis_index("row"), lax.axis_index("sub")
    rows, features = x_ref.shape
    columns = w_ref.shape[1]
    span = columns // CHUNKS
    block = features // row_count
    slab = features // sub_count
    piece = span // row_count

    barrier = pltpu.get_barrier_semaphore()

    def greet_row(peer):
        pl.semaphore_signal(barrier, inc=1, device_id=(peer, sub), device_id_type=MESH)

    def greet_sub(peer):
        pl.semaphore_signal(barrier, inc=1, device_id=(row, peer), device_id_type=MESH)

    for_peers(row, row_count, greet_row)
    for_peers(sub, sub_count, greet_sub)

    turned[...] = nn(x_ref[...], w_ref[...]).T
    slope[...] = nn(u_ref[...], w_ref[...]).T
    xt[...] = x_ref[...].T
    ut[...] = u_ref[...].T

    def rot_copy(h, peer, slot):
        return pltpu.make_async_remote_copy(
            src_ref=rot_out.at[h, pl.ds(pl.multiple_of(peer * block, block), block)],
            dst_ref=rot_got.at[h, slot],
            send_sem=rot_send.at[h, peer],
            recv_sem=rot_recv.at[h, slot],
            device_id=(peer, sub),
            device_id_type=MESH,
        )

    def cg_copy(h, peer, slot):
        return pltpu.make_async_remote_copy(
            src_ref=cg_out.at[h, pl.ds(pl.multiple_of(peer * piece, piece), piece)],
            dst_ref=cg_got.at[h, slot],
            send_sem=cg_send.at[h, peer],
            recv_sem=cg_recv.at[h, slot],
            device_id=(peer, sub),
            device_id_type=MESH,
        )

    def all_copy(h, peer, slot):
        return pltpu.make_async_remote_copy(
            src_ref=cg_sum.at[h],
            dst_ref=cg_all.at[h, slot],
            send_sem=all_send.at[h, peer],
            recv_sem=all_recv.at[h, slot],
            device_id=(peer, sub),
            device_id_type=MESH,
        )

    def in_copy(peer, slot):
        return pltpu.make_async_remote_copy(
            src_ref=in_out.at[pl.ds(pl.multiple_of(peer * slab, slab), slab)],
            dst_ref=in_got.at[slot],
            send_sem=in_send.at[peer],
            recv_sem=in_recv.at[slot],
            device_id=(row, peer),
            device_id_type=MESH,
        )

    def work(h):
        per = span // 8

        def body(i, carry):
            subspaces(
                h * per + i * GROUP,
                book_ref,
                temper_ref,
                turned,
                slope,
                grad,
                recon,
                cg,
            )
            return carry

        lax.fori_loop(0, per // GROUP, body, 0)
        grad_low[pl.ds(h * span, span), :] = grad[pl.ds(h * span, span), :].astype(BF16)

    def send_codes(h):
        if share_codes:
            cg_out[h] = cg[pl.ds(h * span, span), :].astype(BF16)
            for_peers(row, row_count, lambda peer: cg_copy(h, peer, row).start())
        else:
            codes_ref[pl.ds(h * span, span), :] = cg[pl.ds(h * span, span), :]

    def send_rotation(h):
        rot_out[h] = (
            nt(xt[...], grad_low[pl.ds(h * span, span), :])
            + nt(ut[...], recon[pl.ds(h * span, span), :].astype(BF16))
        ).astype(BF16)
        for_peers(row, row_count, lambda peer: rot_copy(h, peer, row).start())

    def finish_codes(h):
        if share_codes:
            own = pl.ds(pl.multiple_of(row * piece, piece), piece)
            for_peers(row, row_count, lambda peer: cg_copy(h, row, peer).wait_recv())
            cg_got[h, row] = cg_out[h, own, :]
            total = cg_got[h, 0].astype(F32)
            for other in range(1, row_count):
                total += cg_got[h, other].astype(F32)
            cg_sum[h] = total.astype(BF16)
            for_peers(row, row_count, lambda peer: all_copy(h, peer, row).start())

    def finish_rotation(h):
        for_peers(row, row_count, lambda peer: rot_copy(h, row, peer).wait_recv())
        rot_got[h, row] = rot_out[h, pl.ds(pl.multiple_of(row * block, block), block), :]
        total = rot_got[h, 0].astype(F32)
        for other in range(1, row_count):
            total += rot_got[h, other].astype(F32)
        rotation_ref[:, pl.ds(h * span, span)] = total

    work(0)
    pl.semaphore_wait(barrier, row_count + sub_count - 2)
    send_codes(0)
    send_rotation(0)
    work(1)
    send_codes(1)
    in_out[...] = nn(w_ref[...], grad_low[...]).astype(BF16)
    for_peers(sub, sub_count, lambda peer: in_copy(peer, sub).start())
    send_rotation(1)
    finish_codes(0)
    finish_codes(1)
    finish_rotation(0)

    for_peers(sub, sub_count, lambda peer: in_copy(sub, peer).wait_recv())
    in_got[sub] = in_out[pl.ds(pl.multiple_of(sub * slab, slab), slab), :]
    total = in_got[0].astype(F32)
    for other in range(1, sub_count):
        total += in_got[other].astype(F32)
    input_ref[...] = total.T.astype(BF16)

    finish_rotation(1)

    if share_codes:
        for h in range(CHUNKS):
            for_peers(row, row_count, lambda peer: all_copy(h, row, peer).wait_recv())
            cg_all[h, row] = cg_sum[h]
            for other in range(row_count):
                codes_ref[pl.ds(h * span + other * piece, piece), :] = cg_all[h, other].astype(F32)

    for_peers(sub, sub_count, lambda peer: in_copy(peer, sub).wait_send())
    for h in range(CHUNKS):
        for_peers(row, row_count, lambda peer: rot_copy(h, peer, row).wait_send())
        if share_codes:
            for_peers(row, row_count, lambda peer: cg_copy(h, peer, row).wait_send())
            for_peers(row, row_count, lambda peer: all_copy(h, peer, row).wait_send())


def on_device(
    feature_vectors, upstream_sensitivity, linear_mapping_matrix, centroid_tables, softness_factor
):
    row_count, sub_count = lax.axis_size("row"), lax.axis_size("sub")
    rows, features = feature_vectors.shape
    columns = linear_mapping_matrix.shape[1]
    subs, width, codes = centroid_tables.shape
    span = columns // CHUNKS
    block = features // row_count
    slab = features // sub_count
    share_codes = span % (16 * row_count) == 0
    piece = span // row_count if share_codes else 16
    row_sems = pltpu.SemaphoreType.DMA((CHUNKS, row_count))
    sub_sems = pltpu.SemaphoreType.DMA((sub_count,))
    vmem = pl.BlockSpec(memory_space=pltpu.VMEM)
    input_grad, rotation_grad, code_grad = pl.pallas_call(
        functools.partial(kernel, row_count, sub_count, share_codes),
        out_shape=(
            jax.ShapeDtypeStruct((rows, slab), BF16),
            jax.ShapeDtypeStruct((block, columns), F32),
            jax.ShapeDtypeStruct((subs * width, codes), F32),
        ),
        in_specs=[vmem, vmem, vmem, vmem, pl.BlockSpec(memory_space=pltpu.SMEM)],
        out_specs=(vmem, vmem, vmem),
        scratch_shapes=[
            pltpu.VMEM((features, rows), BF16),
            pltpu.VMEM((features, rows), BF16),
            pltpu.VMEM((columns, rows), F32),
            pltpu.VMEM((columns, rows), F32),
            pltpu.VMEM((columns, rows), F32),
            pltpu.VMEM((columns, rows), F32),
            pltpu.VMEM((columns, codes), F32),
            pltpu.VMEM((columns, rows), BF16),
            pltpu.VMEM((features, rows), BF16),
            pltpu.VMEM((sub_count, slab, rows), BF16),
            pltpu.VMEM((CHUNKS, features, span), BF16),
            pltpu.VMEM((CHUNKS, row_count, block, span), BF16),
            pltpu.VMEM((CHUNKS, span, codes), BF16),
            pltpu.VMEM((CHUNKS, row_count, piece, codes), BF16),
            pltpu.VMEM((CHUNKS, piece, codes), BF16),
            pltpu.VMEM((CHUNKS, row_count, piece, codes), BF16),
            sub_sems,
            sub_sems,
            row_sems,
            row_sems,
            row_sems,
            row_sems,
            row_sems,
            row_sems,
        ],
        compiler_params=pltpu.CompilerParams(
            collective_id=0, has_side_effects=True, vmem_limit_bytes=48 * 1024 * 1024
        ),
        name="soft_pq_backward",
    )(
        feature_vectors,
        upstream_sensitivity,
        linear_mapping_matrix,
        centroid_tables.reshape(subs * width, codes),
        softness_factor,
    )
    if not share_codes:
        code_grad = lax.psum(code_grad, "row")
    return input_grad, rotation_grad, code_grad.reshape(subs, width, codes)


def solution(mesh):
    return jax.shard_map(
        on_device,
        mesh=mesh,
        in_specs=(P("row", None), P("row", None), P(None, "sub"), P("sub", None, None), P("sub")),
        out_specs=(P("row", "sub"), P("row", "sub"), P("sub", None, None)),
        check_vma=False,
    )
```

profile of v0, /device:TPU:0, one launch (start us, length us, event | category | flops | bytes accessed | tf_op | source)
XLA Modules:
  0.0 36.4 jit_solution(3443631898798141670)
XLA Ops:
  0.6 0.0 copy-start.4
  0.6 0.6 %copy-done.4 = f32[32]{0:T(128)S(1)} copy-done((f32[32]{0:T(128)S(1)}, f32[32]{0:T(128)}, u32[]{:S(2)}) %copy-start.4) | copy-done | bytes 152
  1.3 0.0 copy-start
  1.3 1.0 %copy-done = bf16[256,1024]{1,0:T(8,128)(2,1)S(1)} copy-done((bf16[256,1024]{1,0:T(8,128)(2,1)S(1)}, bf16[256,1024]{1,0:T(8,128)(2,1)}, u32[]{:S(2)}) %copy-start) | copy-done | bytes 524312
  2.3 0.0 copy-start.1
  2.3 1.0 %copy-done.1 = bf16[256,1024]{1,0:T(8,128)(2,1)S(1)} copy-done((bf16[256,1024]{1,0:T(8,128)(2,1)S(1)}, bf16[256,1024]{1,0:T(8,128)(2,1)}, u32[]{:S(2)}) %copy-start.1) | copy-done | bytes 524312
  3.4 0.0 copy-start.2
  3.4 1.0 %copy-done.2 = bf16[1024,256]{1,0:T(8,128)(2,1)S(1)} copy-done((bf16[1024,256]{1,0:T(8,128)(2,1)S(1)}, bf16[1024,256]{1,0:T(8,128)(2,1)}, u32[]{:S(2)}) %copy-start.2) | copy-done | bytes 524312
  4.4 0.0 copy-start.3
  4.4 0.9 %copy-done.3 = f32[32,8,256]{2,1,0:T(8,128)S(1)} copy-done((f32[32,8,256]{2,1,0:T(8,128)S(1)}, f32[32,8,256]{2,1,0:T(8,128)}, u32[]{:S(2)}) %copy-start.3) | copy-done | bytes 262168
  5.4 29.0 %soft_pq_backward.1 = (bf16[256,256]{1,0:T(8,128)(2,1)S(1)}, f32[128,256]{1,0:T(8,128)S(1)}, f32[256,256]{1,0:T(8,128)S(1)}) custom-call(bf16[256,1024]{1,0:T(8,128)(2,1)S(1)} %copy-done, bf16[256,1024]{1,0:T(8,128)(2,1)S(1)} %copy-done.1, bf16[1024,256]{1,0:T(8,128)(2,1)S(1)} %copy-done.2, f32[256,256]{1,0:T(8,128)S(1)} %bitcast.3, f32[32]{0:T(128)S(1)} %copy-done.4), custom_call_target="tpu_custom_call" | custom-call | tf_op jit(solution)/shard_map/soft_pq_backward/pallas_call | solution.py:327
  34.4 0.7 %copy.11 = bf16[256,256]{1,0:T(8,128)(2,1)} copy(bf16[256,256]{1,0:T(8,128)(2,1)S(1)} %get-tuple-element.12) | data formatting | bytes 262144
  35.0 0.7 %copy.12 = f32[128,256]{1,0:T(8,128)} copy(f32[128,256]{1,0:T(8,128)S(1)} %get-tuple-element.13) | data formatting | bytes 262144
  35.7 0.7 %copy.13 = f32[32,8,256]{2,1,0:T(8,128)} copy(f32[32,8,256]{2,1,0:T(8,128)S(1)} %bitcast.2) | data formatting | bytes 524288
Async XLA Ops:
  0.6 0.7 %copy-start.4 = (f32[32]{0:T(128)S(1)}, f32[32]{0:T(128)}, u32[]{:S(2)}) copy-start(f32[32]{0:T(128)} %temper_ref.1) | copy-start | bytes 388
  1.3 1.0 %copy-start = (bf16[256,1024]{1,0:T(8,128)(2,1)S(1)}, bf16[256,1024]{1,0:T(8,128)(2,1)}, u32[]{:S(2)}) copy-start(bf16[256,1024]{1,0:T(8,128)(2,1)} %x_ref.1) | copy-start | bytes 1572868
  2.3 1.0 %copy-start.1 = (bf16[256,1024]{1,0:T(8,128)(2,1)S(1)}, bf16[256,1024]{1,0:T(8,128)(2,1)}, u32[]{:S(2)}) copy-start(bf16[256,1024]{1,0:T(8,128)(2,1)} %u_ref.1) | copy-start | bytes 1572868
  3.4 1.0 %copy-start.2 = (bf16[1024,256]{1,0:T(8,128)(2,1)S(1)}, bf16[1024,256]{1,0:T(8,128)(2,1)}, u32[]{:S(2)}) copy-start(bf16[1024,256]{1,0:T(8,128)(2,1)} %w_ref.1) | copy-start | bytes 1572868
  4.4 0.9 %copy-start.3 = (f32[32,8,256]{2,1,0:T(8,128)S(1)}, f32[32,8,256]{2,1,0:T(8,128)}, u32[]{:S(2)}) copy-start(f32[32,8,256]{2,1,0:T(8,128)} %param.8) | copy-start | bytes 786436
where the time goes:
time: 36.7 us; the launch traced here: 36.4 us
  Pallas kernels  29 us (79%)
  local copies, waits for them, and re-layouts  6.74 us (18%)
  between operations  0.65 us (2%)
    pallas_call x1, Pallas kernels, on_device(): pl.pallas_call(functools.partial(kernel, row_count, sub_count, share_code...  29 us
    unnamed x13, local copies, waits for them, and re-layouts  6.74 us

commit v1 on v0

v1 whole, which is shorter than its diff:
```python
import functools

import jax
import jax.numpy as jnp
from jax import lax
from jax.experimental import pallas as pl
from jax.experimental.pallas import tpu as pltpu
from jax.sharding import PartitionSpec as P

MESH = pl.DeviceIdType.MESH
LOG2E = 1.4426950408889634
CHUNKS = 4
GROUP = 4
F32 = jnp.float32
BF16 = jnp.bfloat16


def nn(a, b):
    return lax.dot_general(a, b, (((1,), (0,)), ((), ())), preferred_element_type=F32)


def nt(a, b):
    return lax.dot_general(a, b, (((1,), (1,)), ((), ())), preferred_element_type=F32)


def low(x):
    return x.astype(BF16).astype(F32)


def split3(x):
    first = low(x)
    rest = x - first
    second = low(rest)
    return first, second, low(rest - second)


def split2(x):
    first = low(x)
    return first, low(x - first)


def for_peers(me, count, body):
    if count <= 8:
        for step in range(1, count):
            body(lax.rem(me + step, count))
    else:

        def run(step, carry):
            body(lax.rem(me + step, count))
            return carry

        lax.fori_loop(1, count, run, 0)


def subspaces(first, book_ref, temper_ref, turned_ref, slope_ref, grad_ref, recon_ref, cg_ref):
    width = 8
    codes = book_ref.shape[1]
    rows = turned_ref.shape[1]
    at = [pl.ds(pl.multiple_of((first + j) * width, width), width) for j in range(GROUP)]
    sub_k = lax.broadcasted_iota(jnp.int32, (width, codes), 0)
    sub_n = lax.broadcasted_iota(jnp.int32, (width, rows), 0)
    none_k = jnp.zeros((width, codes), F32)
    none_n = jnp.zeros((width, rows), F32)
    ones_n = jnp.where(sub_n < 3, 1.0, 0.0).astype(F32)
    one_k = jnp.where(sub_k == 0, 1.0, 0.0).astype(F32)
    both, books = [], []
    for j in range(GROUP):
        temper = temper_ref[first + j]
        c, z, g = book_ref[at[j], :], turned_ref[at[j], :], slope_ref[at[j], :]
        c1, c2, c3 = split3(c)
        square = jnp.sum(c * c, 0, keepdims=True) * (-LOG2E / jnp.full((1, codes), temper, F32))
        q1, q2, q3 = split3(square)
        squares = jnp.where(
            sub_k == 0, q1, jnp.where(sub_k == 1, q2, jnp.where(sub_k == 2, q3, 0.0))
        )
        left = jnp.concatenate([c1, c2, c3, c1, c2, c1, squares, none_k], 0).astype(BF16).T
        z1, z2, z3 = split3(z * (2.0 * LOG2E / jnp.full((1, rows), temper, F32)))
        g1, g2, g3 = split3(g)
        right = jnp.concatenate(
            [
                jnp.concatenate([z1, z1, z1, z2, z2, z3, ones_n, none_n], 0).astype(BF16),
                jnp.concatenate([g1, g1, g1, g2, g2, g3, none_n, none_n], 0).astype(BF16),
            ],
            1,
        )
        both.append(nn(left, right))
        books.append(jnp.concatenate([c1, c2, one_k, none_k], 0).astype(BF16))
    exps, exps_low = [], []
    for j in range(GROUP):
        s = both[j][:, :rows]
        e = jnp.exp2(s - jnp.max(s, 0, keepdims=True))
        exps.append(e)
        exps_low.append(e.astype(BF16))
    sums = [nn(books[j], exps_low[j]) for j in range(GROUP)]
    slopes, scales, backs = [], [], []
    for j in range(GROUP):
        back = 1.0 / sums[j][16:17]
        recon = (sums[j][0:8] + sums[j][8:16]) * back
        recon_ref[at[j], :] = recon
        mean = jnp.sum(slope_ref[at[j], :] * recon, 0, keepdims=True)
        slopes.append((exps[j] * (both[j][:, rows:] - mean)).astype(BF16))
        backs.append(back)
        scales.append(back * (2.0 / jnp.full((1, rows), temper_ref[first + j], F32)))
    for j in range(GROUP):
        c, z, g = book_ref[at[j], :], turned_ref[at[j], :], slope_ref[at[j], :]
        w = nn(books[j], slopes[j])
        total = w[16:17] * scales[j]
        grad_ref[at[j], :] = (w[0:8] + w[8:16]) * scales[j] - z * total
        a1, a2 = split2(g * backs[j])
        b1, b2 = split2(z * scales[j])
        t1, t2 = split2(scales[j])
        tops = jnp.where(sub_n == 0, t1, jnp.where(sub_n == 1, t2, 0.0))
        from_assign = nt(jnp.concatenate([a1, a2], 0).astype(BF16), exps_low[j])
        from_weight = nt(jnp.concatenate([b1, b2, tops, none_n], 0).astype(BF16), slopes[j])
        cg_ref[at[j], :] = (
            (from_assign[0:8] + from_assign[8:16])
            + (from_weight[0:8] + from_weight[8:16])
            - c * (from_weight[16:17] + from_weight[17:18])
        )


def kernel(
    row_count,
    sub_count,
    share,
    x_hbm,
    u_hbm,
    w_hbm,
    book_hbm,
    temper_hbm,
    input_ref,
    rotation_ref,
    codes_ref,
    x_ref,
    u_ref,
    w_ref,
    book_ref,
    temper_ref,
    turned,
    slope,
    grad,
    recon,
    cg,
    w_all,
    g_all,
    rot_sum,
    pair_out,
    pair_got,
    rest_out,
    rest_got,
    code_sum,
    code_all,
    load_sems,
    w_send,
    w_recv,
    g_send,
    g_recv,
    pair_send,
    pair_recv,
    rest_send,
    rest_recv,
    code_send,
    code_recv,
):
    row, sub = lax.axis_index("row"), lax.axis_index("sub")
    rows, features = x_ref.shape
    columns = w_ref.shape[1]
    codes = book_ref.shape[1]
    span = columns // CHUNKS
    slab = features // sub_count
    rests = row_count // 2
    bit, rest = lax.rem(row, 2), row // 2
    partner = rest * 2 + (1 - bit)
    block = features // row_count
    half = codes // 2
    piece = span // rests if share else 16

    loads = [
        pltpu.make_async_copy(src, dst, load_sems.at[i])
        for i, (src, dst) in enumerate(
            [
                (x_hbm, x_ref),
                (w_hbm, w_ref),
                (u_hbm, u_ref),
                (book_hbm, book_ref),
                (temper_hbm, temper_ref),
            ]
        )
    ]
    for load in loads:
        load.start()

    barrier = pltpu.get_barrier_semaphore()

    def greet_row(peer):
        pl.semaphore_signal(barrier, inc=1, device_id=(peer, sub), device_id_type=MESH)

    def greet_sub(peer):
        pl.semaphore_signal(barrier, inc=1, device_id=(row, peer), device_id_type=MESH)

    if share:
        for_peers(row, row_count, greet_row)
    for_peers(sub, sub_count, greet_sub)

    def remote(src, dst, send, recv, device):
        return pltpu.make_async_remote_copy(
            src_ref=src,
            dst_ref=dst,
            send_sem=send,
            recv_sem=recv,
            device_id=device,
            device_id_type=MESH,
        )

    def w_copy(peer, slot):
        at = pl.ds(pl.multiple_of(peer * slab, slab), slab)
        return remote(
            w_ref.at[at], w_all.at[slot], w_send.at[peer], w_recv.at[slot], (row, peer)
        )

    def g_copy(h, peer, slot):
        at = pl.ds(h * span, span)
        return remote(
            g_all.at[slot, at],
            g_all.at[slot, at],
            g_send.at[h, peer],
            g_recv.at[h, slot],
            (row, peer),
        )

    def pair_copy(h):
        return remote(
            pair_out.at[h, 1 - bit], pair_got.at[h], pair_send.at[h], pair_recv.at[h], (partner, sub)
        )

    def rest_copy(h, peer, slot):
        return remote(
            rest_out.at[h, peer],
            rest_got.at[h, slot],
            rest_send.at[h, peer],
            rest_recv.at[h, slot],
            (peer * 2 + bit, sub),
        )

    def code_copy(h, peer, slot):
        return remote(
            code_sum.at[h],
            code_all.at[h, slot],
            code_send.at[h, peer],
            code_recv.at[h, slot],
            (peer, sub),
        )

    def work(h):
        per = span // 8

        def body(i, carry):
            subspaces(
                h * per + i * GROUP, book_ref, temper_ref, turned, slope, grad, recon, cg
            )
            return carry

        lax.fori_loop(0, per // GROUP, body, 0)

    def send_grad(h):
        at = pl.ds(h * span, span)
        g_all[sub, at, :] = grad[at, :].astype(BF16)
        for_peers(sub, sub_count, lambda peer: g_copy(h, peer, sub).start())

    def send_pair(h):
        at = pl.ds(h * span, span)
        local = nn(g_all[sub, at, :], x_ref[...]) + nn(recon[at, :].astype(BF16), u_ref[...])
        if share:
            for peer in range(rests):
                for side in range(2):
                    start = (peer * 2 + side) * block
                    pair_out[h, side, peer] = local[:, start : start + block].astype(BF16)
            for side in range(2):
                pair_out[h, side, rests] = cg[at, side * half : (side + 1) * half].astype(BF16)
            pair_copy(h).start()
        else:
            rotation_ref[at, :] = local
            codes_ref[at, :] = cg[at, :]

    def send_rest(h):
        if share:
            pair_copy(h).wait_recv()
            for peer in range(rests):
                rest_out[h, peer, :span, :] = (
                    pair_out[h, bit, peer].astype(F32) + pair_got[h, peer].astype(F32)
                ).astype(BF16)
                at = pl.ds(peer * piece, piece)
                rest_out[h, peer, span:, :] = (
                    pair_out[h, bit, rests, at].astype(F32) + pair_got[h, rests, at].astype(F32)
                ).astype(BF16)
            for_peers(rest, rests, lambda peer: rest_copy(h, peer, rest).start())

    def finish_rest(h):
        if share:
            for_peers(rest, rests, lambda peer: rest_copy(h, rest, peer).wait_recv())
            rest_got[h, rest] = rest_out[h, rest]
            total = rest_got[h, 0, span:, :].astype(F32)
            for other in range(1, rests):
                total += rest_got[h, other, span:, :].astype(F32)
            code_sum[h] = total.astype(BF16)
            for_peers(row, row_count, lambda peer: code_copy(h, peer, row).start())
            total = rest_got[h, 0, :span, :].astype(F32)
            for other in range(1, rests):
                total += rest_got[h, other, :span, :].astype(F32)
            rot_sum[pl.ds(h * span, span), :] = total

    def finish_codes(h):
        if share:
            for_peers(row, row_count, lambda peer: code_copy(h, row, peer).wait_recv())
            code_all[h, row] = code_sum[h]
            for other in range(row_count):
                codes_ref[
                    pl.ds(h * span + other // 2 * piece, piece),
                    other % 2 * half : (other % 2 + 1) * half,
                ] = code_all[h, other].astype(F32)

    loads[0].wait()
    loads[1].wait()
    turned[...] = nn(x_ref[...], w_ref[...]).T
    loads[2].wait()
    slope[...] = nn(u_ref[...], w_ref[...]).T
    loads[3].wait()
    loads[4].wait()
    pl.semaphore_wait(barrier, sub_count - 1 + (row_count - 1 if share else 0))
    for_peers(sub, sub_count, lambda peer: w_copy(peer, sub).start())

    for h in range(CHUNKS):
        work(h)
        send_grad(h)
        send_pair(h)
        if h >= 1:
            send_rest(h - 1)
        if h >= 2:
            finish_rest(h - 2)
    send_rest(CHUNKS - 1)
    finish_rest(CHUNKS - 2)

    for_peers(sub, sub_count, lambda peer: w_copy(sub, peer).wait_recv())
    w_all[sub] = w_ref[pl.ds(pl.multiple_of(sub * slab, slab), slab), :]
    for h in range(CHUNKS):
        for_peers(sub, sub_count, lambda peer: g_copy(h, sub, peer).wait_recv())
    total = nn(w_all[0], g_all[0]).astype(BF16).astype(F32)
    for other in range(1, sub_count):
        total += nn(w_all[other], g_all[other]).astype(BF16).astype(F32)
    input_ref[...] = total.T.astype(BF16)

    finish_rest(CHUNKS - 1)
    if share:
        rotation_ref[...] = rot_sum[...].T
    for h in range(CHUNKS):
        finish_codes(h)

    for_peers(sub, sub_count, lambda peer: w_copy(peer, sub).wait_send())
    for h in range(CHUNKS):
        for_peers(sub, sub_count, lambda peer: g_copy(h, peer, sub).wait_send())
        if share:
            pair_copy(h).wait_send()
            for_peers(rest, rests, lambda peer: rest_copy(h, peer, rest).wait_send())
            for_peers(row, row_count, lambda peer: code_copy(h, peer, row).wait_send())


def store_kernel(a_ref, b_ref, c_ref, a_out, b_out, c_out, sems):
    stores = [
        pltpu.make_async_copy(src, dst, sems.at[i])
        for i, (src, dst) in enumerate([(a_ref, a_out), (b_ref, b_out), (c_ref, c_out)])
    ]
    for store in stores:
        store.start()
    for store in stores:
        store.wait()


def on_device(
    feature_vectors, upstream_sensitivity, linear_mapping_matrix, centroid_tables, softness_factor
):
    row_count, sub_count = lax.axis_size("row"), lax.axis_size("sub")
    rows, features = feature_vectors.shape
    columns = linear_mapping_matrix.shape[1]
    subs, width, codes = centroid_tables.shape
    span = columns // CHUNKS
    block = features // row_count
    slab = features // sub_count
    rests = row_count // 2
    share = (
        row_count % 2 == 0
        and row_count <= 8
        and block == codes // 2
        and block % 128 == 0
        and span % (16 * rests) == 0
    )
    pieces = rests if share else 1
    piece = span // pieces
    lanes = block if share else 128
    dma = pltpu.SemaphoreType.DMA
    vmem = pl.BlockSpec(memory_space=pltpu.VMEM)
    hbm = pl.BlockSpec(memory_space=pltpu.HBM)
    rotation_shape = (block, columns) if share else (columns, features)
    results = pl.pallas_call(
        functools.partial(kernel, row_count, sub_count, share),
        out_shape=(
            jax.ShapeDtypeStruct((rows, slab), BF16),
            jax.ShapeDtypeStruct(rotation_shape, F32),
            jax.ShapeDtypeStruct((subs * width, codes), F32),
        ),
        in_specs=[hbm, hbm, hbm, hbm, hbm],
        out_specs=(vmem, vmem, vmem),
        scratch_shapes=[
            pltpu.VMEM((rows, features), BF16),
            pltpu.VMEM((rows, features), BF16),
            pltpu.VMEM((features, columns), BF16),
            pltpu.VMEM((columns, codes), F32),
            pltpu.SMEM((subs,), F32),
            pltpu.VMEM((columns, rows), F32),
            pltpu.VMEM((columns, rows), F32),
            pltpu.VMEM((columns, rows), F32),
            pltpu.VMEM((columns, rows), F32),
            pltpu.VMEM((columns, codes), F32),
            pltpu.VMEM((sub_count, slab, columns), BF16),
            pltpu.VMEM((sub_count, columns, rows), BF16),
            pltpu.VMEM((columns, lanes), F32),
            pltpu.VMEM((CHUNKS, 2, pieces + 1, span, lanes), BF16),
            pltpu.VMEM((CHUNKS, pieces + 1, span, lanes), BF16),
            pltpu.VMEM((CHUNKS, pieces, span + piece, lanes), BF16),
            pltpu.VMEM((CHUNKS, pieces, span + piece, lanes), BF16),
            pltpu.VMEM((CHUNKS, piece, lanes), BF16),
            pltpu.VMEM((CHUNKS, row_count, piece, lanes), BF16),
            dma((5,)),
            dma((sub_count,)),
            dma((sub_count,)),
            dma((CHUNKS, sub_count)),
            dma((CHUNKS, sub_count)),
            dma((CHUNKS,)),
            dma((CHUNKS,)),
            dma((CHUNKS, pieces)),
            dma((CHUNKS, pieces)),
            dma((CHUNKS, row_count)),
            dma((CHUNKS, row_count)),
        ],
        compiler_params=pltpu.CompilerParams(
            collective_id=0, has_side_effects=True, vmem_limit_bytes=54700 * 1024
        ),
        name="soft_pq_backward",
    )(
        feature_vectors,
        upstream_sensitivity,
        linear_mapping_matrix,
        centroid_tables.reshape(subs * width, codes),
        softness_factor,
    )
    if share:
        results = pl.pallas_call(
            store_kernel,
            out_shape=tuple(jax.ShapeDtypeStruct(r.shape, r.dtype) for r in results),
            in_specs=[vmem, vmem, vmem],
            out_specs=(hbm, hbm, hbm),
            scratch_shapes=[dma((3,))],
            name="store_results",
        )(*results)
        input_grad, rotation_grad, code_grad = results
    else:
        input_grad, rotation_grad, code_grad = results
        rotation_grad = lax.psum_scatter(rotation_grad.T, "row", scatter_dimension=0, tiled=True)
        code_grad = lax.psum(code_grad, "row")
    return input_grad, rotation_grad, code_grad.reshape(subs, width, codes)


def solution(mesh):
    return jax.shard_map(
        on_device,
        mesh=mesh,
        in_specs=(P("row", None), P("row", None), P(None, "sub"), P("sub", None, None), P("sub")),
        out_specs=(P("row", "sub"), P("row", "sub"), P("sub", None, None)),
        check_vma=False,
    )
```

time: 36.7 us -> 36.7 us (level)
  Pallas kernels: 29 us -> 33.2 us
  local copies, waits for them, and re-layouts: 6.74 us -> 2.63 us
    pallas_call x1 -> x2, Pallas kernels: 29 us -> 33.2 us  [the longest x1 31.3 us: on_device(): pl.pallas_call(functools.partial(kernel, row_count, sub_count, share), ou...]
    unnamed x13 -> x8, local copies, waits for them, and re-layouts: 6.74 us -> 2.63 us
where the time goes in v1:
time: 36.7 us; the launch traced here: 36.5 us
  Pallas kernels  33.2 us (90%)
  local copies, waits for them, and re-layouts  2.63 us (7%)
  between operations  0.66 us (2%)
    pallas_call x1, Pallas kernels, on_device(): pl.pallas_call(functools.partial(kernel, row_count, sub_count, share), ou...  31.3 us
    unnamed x8, local copies, waits for them, and re-layouts  2.63 us
    pallas_call x1, Pallas kernels, on_device(): pl.pallas_call(store_kernel, out_shape=tuple((jax.ShapeDtypeStruct(r.shap...  1.9 us

profile of v1, /device:TPU:0, one launch (start us, length us, event | category | flops | bytes accessed | tf_op | source)
XLA Modules:
  0.0 36.5 jit_solution(13847251810839233618)
XLA Ops:
  0.6 0.0 copy-start.3
  0.6 0.6 %copy-done.3 = f32[32]{0:T(128)S(1)} copy-done((f32[32]{0:T(128)S(1)}, f32[32]{0:T(128)}, u32[]{:S(2)}) %copy-start.3) | copy-done | bytes 152
  1.3 31.3 %soft_pq_backward.1 = (bf16[256,256]{1,0:T(8,128)(2,1)S(1)}, f32[128,256]{1,0:T(8,128)S(1)}, f32[256,256]{1,0:T(8,128)S(1)}) custom-call(bf16[256,1024]{1,0:T(8,128)(2,1)} %x_hbm.1, bf16[256,1024]{1,0:T(8,128)(2,1)} %u_hbm.1, bf16[1024,256]{1,0:T(8,128)(2,1)} %w_hbm.1, f32[256,256]{1,0:T(8,128)} %bitcast.2, f32[32]{0:T(128)S(1)} %copy-done.3), custom_call_target="tpu_custom_call" | custom-call | tf_op jit(solution)/shard_map/soft_pq_backward/pallas_call | solution.py:403
  32.6 0.0 copy-start
  32.6 0.7 %copy-done = f32[256,256]{1,0:T(8,128)} copy-done((f32[256,256]{1,0:T(8,128)}, f32[256,256]{1,0:T(8,128)S(1)}, u32[]{:S(2)}) %copy-start) | copy-done | bytes 262168
  33.3 0.0 copy-start.1
  33.3 0.6 %copy-done.1 = bf16[256,256]{1,0:T(8,128)(2,1)} copy-done((bf16[256,256]{1,0:T(8,128)(2,1)}, bf16[256,256]{1,0:T(8,128)(2,1)S(1)}, u32[]{:S(2)}) %copy-start.1) | copy-done | bytes 131096
  34.0 0.0 copy-start.2
  34.0 0.6 %copy-done.2 = f32[128,256]{1,0:T(8,128)} copy-done((f32[128,256]{1,0:T(8,128)}, f32[128,256]{1,0:T(8,128)S(1)}, u32[]{:S(2)}) %copy-start.2) | copy-done | bytes 131096
  34.6 1.9 %store_results.1 = (bf16[256,256]{1,0:T(8,128)(2,1)}, f32[128,256]{1,0:T(8,128)}, f32[256,256]{1,0:T(8,128)}) custom-call(bf16[256,256]{1,0:T(8,128)(2,1)} %copy-done.1, f32[128,256]{1,0:T(8,128)} %copy-done.2, f32[256,256]{1,0:T(8,128)} %copy-done), custom_call_target="tpu_custom_call" | custom-call | tf_op jit(solution)/shard_map/store_results/pallas_call | solution.py:456
Async XLA Ops:
  0.6 0.7 %copy-start.3 = (f32[32]{0:T(128)S(1)}, f32[32]{0:T(128)}, u32[]{:S(2)}) copy-start(f32[32]{0:T(128)} %temper_hbm.1) | copy-start | bytes 388
  32.6 0.7 %copy-start = (f32[256,256]{1,0:T(8,128)}, f32[256,256]{1,0:T(8,128)S(1)}, u32[]{:S(2)}) copy-start(f32[256,256]{1,0:T(8,128)S(1)} %get-tuple-element.11.c_ref) | copy-start | bytes 786436
  33.3 0.6 %copy-start.1 = (bf16[256,256]{1,0:T(8,128)(2,1)}, bf16[256,256]{1,0:T(8,128)(2,1)S(1)}, u32[]{:S(2)}) copy-start(bf16[256,256]{1,0:T(8,128)(2,1)S(1)} %get-tuple-element.9.a_ref) | copy-start | bytes 393220
  34.0 0.6 %copy-start.2 = (f32[128,256]{1,0:T(8,128)}, f32[128,256]{1,0:T(8,128)S(1)}, u32[]{:S(2)}) copy-start(f32[128,256]{1,0:T(8,128)S(1)} %get-tuple-element.10.b_ref) | copy-start | bytes 393220

commit v2 on v1

--- a/solution.py
+++ b/solution.py
@@ -63,7 +63,7 @@
     none_n = jnp.zeros((width, rows), F32)
     ones_n = jnp.where(sub_n < 3, 1.0, 0.0).astype(F32)
     one_k = jnp.where(sub_k == 0, 1.0, 0.0).astype(F32)
-    both, books = [], []
+    books, lefts, rights = [], [], []
     for j in range(GROUP):
         temper = temper_ref[first + j]
         c, z, g = book_ref[at[j], :], turned_ref[at[j], :], slope_ref[at[j], :]
@@ -73,18 +73,27 @@
         squares = jnp.where(
             sub_k == 0, q1, jnp.where(sub_k == 1, q2, jnp.where(sub_k == 2, q3, 0.0))
         )
-        left = jnp.concatenate([c1, c2, c3, c1, c2, c1, squares, none_k], 0).astype(BF16).T
+        lefts.append([c1, c2, c3, c1, c2, c1, squares, none_k])
         z1, z2, z3 = split3(z * (2.0 * LOG2E / jnp.full((1, rows), temper, F32)))
         g1, g2, g3 = split3(g)
-        right = jnp.concatenate(
-            [
-                jnp.concatenate([z1, z1, z1, z2, z2, z3, ones_n, none_n], 0).astype(BF16),
-                jnp.concatenate([g1, g1, g1, g2, g2, g3, none_n, none_n], 0).astype(BF16),
-            ],
-            1,
-        )
-        both.append(nn(left, right))
+        empty = [none_n] * 8
+        for_z = [z1, z1, z1, z2, z2, z3, ones_n, none_n]
+        for_g = [g1, g1, g1, g2, g2, g3, none_n, none_n]
+        rights.append(
+            jnp.concatenate(
+                [
+                    jnp.concatenate(part + empty if j % 2 == 0 else empty + part, 0).astype(BF16)
+                    for part in (for_z, for_g)
+                ],
+                1,
+            )
+        )
         books.append(jnp.concatenate([c1, c2, one_k, none_k], 0).astype(BF16))
+    both = []
+    for j in range(0, GROUP, 2):
+        left = jnp.concatenate(lefts[j] + lefts[j + 1], 0).astype(BF16).T
+        both.append(nn(left, rights[j]))
+        both.append(nn(left, rights[j + 1]))
     exps, exps_low = [], []
     for j in range(GROUP):
         s = both[j][:, :rows]
@@ -92,31 +101,43 @@
         exps.append(e)
         exps_low.append(e.astype(BF16))
     sums = [nn(books[j], exps_low[j]) for j in range(GROUP)]
-    slopes, scales, backs = [], [], []
+    slopes, scales, to_assign, to_weight = [], [], [], []
     for j in range(GROUP):
+        z, g = turned_ref[at[j], :], slope_ref[at[j], :]
         back = 1.0 / sums[j][16:17]
         recon = (sums[j][0:8] + sums[j][8:16]) * back
         recon_ref[at[j], :] = recon
-        mean = jnp.sum(slope_ref[at[j], :] * recon, 0, keepdims=True)
+        mean = jnp.sum(g * recon, 0, keepdims=True)
         slopes.append((exps[j] * (both[j][:, rows:] - mean)).astype(BF16))
-        backs.append(back)
-        scales.append(back * (2.0 / jnp.full((1, rows), temper_ref[first + j], F32)))
+        scale = back * (2.0 / jnp.full((1, rows), temper_ref[first + j], F32))
+        scales.append(scale)
+        a1, a2 = split2(g * back)
+        b1, b2 = split2(z * scale)
+        t1, t2 = split2(scale)
+        tops = jnp.where(sub_n == 0, t1, jnp.where(sub_n == 1, t2, 0.0))
+        to_assign += [a1, a2, none_n, none_n]
+        to_weight += [b1, b2, tops, none_n]
+    ws = [nn(books[j], slopes[j]) for j in range(GROUP)]
+    assign_side = jnp.concatenate(to_assign, 0).astype(BF16).T
+    weight_side = jnp.concatenate(to_weight, 0).astype(BF16).T
+    owner = lax.broadcasted_iota(jnp.int32, (rows, 32 * GROUP), 1) // 32
+    nothing = jnp.zeros((rows, 32 * GROUP), BF16)
+    stacked = jnp.concatenate(exps_low + slopes, 1)
+    weights = jnp.concatenate(
+        [
+            jnp.where(owner == j, side, nothing)
+            for side in (assign_side, weight_side)
+            for j in range(GROUP)
+        ],
+        0,
+    )
+    sides = nn(stacked, weights).T
     for j in range(GROUP):
-        c, z, g = book_ref[at[j], :], turned_ref[at[j], :], slope_ref[at[j], :]
-        w = nn(books[j], slopes[j])
-        total = w[16:17] * scales[j]
-        grad_ref[at[j], :] = (w[0:8] + w[8:16]) * scales[j] - z * total
-        a1, a2 = split2(g * backs[j])
-        b1, b2 = split2(z * scales[j])
-        t1, t2 = split2(scales[j])
-        tops = jnp.where(sub_n == 0, t1, jnp.where(sub_n == 1, t2, 0.0))
-        from_assign = nt(jnp.concatenate([a1, a2], 0).astype(BF16), exps_low[j])
-        from_weight = nt(jnp.concatenate([b1, b2, tops, none_n], 0).astype(BF16), slopes[j])
-        cg_ref[at[j], :] = (
-            (from_assign[0:8] + from_assign[8:16])
-            + (from_weight[0:8] + from_weight[8:16])
-            - c * (from_weight[16:17] + from_weight[17:18])
-        )
+        c, z = book_ref[at[j], :], turned_ref[at[j], :]
+        total = ws[j][16:17] * scales[j]
+        grad_ref[at[j], :] = (ws[j][0:8] + ws[j][8:16]) * scales[j] - z * total
+        mine = sides[32 * j : 32 * j + 32]
+        cg_ref[at[j], :] = mine[0:8] + mine[8:16] - c * (mine[16:17] + mine[17:18])
 
 
 def kernel(
@@ -128,14 +149,17 @@
     w_hbm,
     book_hbm,
     temper_hbm,
-    input_ref,
-    rotation_ref,
-    codes_ref,
+    input_hbm,
+    rotation_hbm,
+    codes_hbm,
     x_ref,
     u_ref,
     w_ref,
     book_ref,
     temper_ref,
+    input_ref,
+    rotation_ref,
+    codes_ref,
     turned,
     slope,
     grad,
@@ -151,6 +175,7 @@
     code_sum,
     code_all,
     load_sems,
+    store_sems,
     w_send,
     w_recv,
     g_send,
@@ -190,6 +215,13 @@
     for load in loads:
         load.start()
 
+    stores = [
+        pltpu.make_async_copy(src, dst, store_sems.at[i])
+        for i, (src, dst) in enumerate(
+            [(input_ref, input_hbm), (rotation_ref, rotation_hbm), (codes_ref, codes_hbm)]
+        )
+    ]
+
     barrier = pltpu.get_barrier_semaphore()
 
     def greet_row(peer):
@@ -219,7 +251,7 @@
         )
 
     def g_copy(h, peer, slot):
-        at = pl.ds(h * span, span)
+        at = pl.ds(pl.multiple_of(h * span, span), span)
         return remote(
             g_all.at[slot, at],
             g_all.at[slot, at],
@@ -263,12 +295,12 @@
         lax.fori_loop(0, per // GROUP, body, 0)
 
     def send_grad(h):
-        at = pl.ds(h * span, span)
+        at = pl.ds(pl.multiple_of(h * span, span), span)
         g_all[sub, at, :] = grad[at, :].astype(BF16)
         for_peers(sub, sub_count, lambda peer: g_copy(h, peer, sub).start())
 
     def send_pair(h):
-        at = pl.ds(h * span, span)
+        at = pl.ds(pl.multiple_of(h * span, span), span)
         local = nn(g_all[sub, at, :], x_ref[...]) + nn(recon[at, :].astype(BF16), u_ref[...])
         if share:
             for peer in range(rests):
@@ -307,7 +339,7 @@
             total = rest_got[h, 0, :span, :].astype(F32)
             for other in range(1, rests):
                 total += rest_got[h, other, :span, :].astype(F32)
-            rot_sum[pl.ds(h * span, span), :] = total
+            rot_sum[pl.ds(pl.multiple_of(h * span, span), span), :] = total
 
     def finish_codes(h):
         if share:
@@ -329,14 +361,15 @@
     pl.semaphore_wait(barrier, sub_count - 1 + (row_count - 1 if share else 0))
     for_peers(sub, sub_count, lambda peer: w_copy(peer, sub).start())
 
-    for h in range(CHUNKS):
+    def chunk(h, carry):
         work(h)
         send_grad(h)
         send_pair(h)
-        if h >= 1:
-            send_rest(h - 1)
-        if h >= 2:
-            finish_rest(h - 2)
+        pl.when(h >= 1)(lambda: send_rest(h - 1))
+        pl.when(h >= 2)(lambda: finish_rest(h - 2))
+        return carry
+
+    lax.fori_loop(0, CHUNKS, chunk, 0)
     send_rest(CHUNKS - 1)
     finish_rest(CHUNKS - 2)
 
@@ -348,12 +381,15 @@
     for other in range(1, sub_count):
         total += nn(w_all[other], g_all[other]).astype(BF16).astype(F32)
     input_ref[...] = total.T.astype(BF16)
+    stores[0].start()
 
     finish_rest(CHUNKS - 1)
     if share:
         rotation_ref[...] = rot_sum[...].T
+    stores[1].start()
     for h in range(CHUNKS):
         finish_codes(h)
+    stores[2].start()
 
     for_peers(sub, sub_count, lambda peer: w_copy(peer, sub).wait_send())
     for h in range(CHUNKS):
@@ -362,15 +398,6 @@
             pair_copy(h).wait_send()
             for_peers(rest, rests, lambda peer: rest_copy(h, peer, rest).wait_send())
             for_peers(row, row_count, lambda peer: code_copy(h, peer, row).wait_send())
-
-
-def store_kernel(a_ref, b_ref, c_ref, a_out, b_out, c_out, sems):
-    stores = [
-        pltpu.make_async_copy(src, dst, sems.at[i])
-        for i, (src, dst) in enumerate([(a_ref, a_out), (b_ref, b_out), (c_ref, c_out)])
-    ]
-    for store in stores:
-        store.start()
     for store in stores:
         store.wait()
 
@@ -397,7 +424,6 @@
     piece = span // pieces
     lanes = block if share else 128
     dma = pltpu.SemaphoreType.DMA
-    vmem = pl.BlockSpec(memory_space=pltpu.VMEM)
     hbm = pl.BlockSpec(memory_space=pltpu.HBM)
     rotation_shape = (block, columns) if share else (columns, features)
     results = pl.pallas_call(
@@ -408,13 +434,16 @@
             jax.ShapeDtypeStruct((subs * width, codes), F32),
         ),
         in_specs=[hbm, hbm, hbm, hbm, hbm],
-        out_specs=(vmem, vmem, vmem),
+        out_specs=(hbm, hbm, hbm),
         scratch_shapes=[
             pltpu.VMEM((rows, features), BF16),
             pltpu.VMEM((rows, features), BF16),
             pltpu.VMEM((features, columns), BF16),
             pltpu.VMEM((columns, codes), F32),
             pltpu.SMEM((subs,), F32),
+            pltpu.VMEM((rows, slab), BF16),
+            pltpu.VMEM(rotation_shape, F32),
+            pltpu.VMEM((subs * width, codes), F32),
             pltpu.VMEM((columns, rows), F32),
             pltpu.VMEM((columns, rows), F32),
             pltpu.VMEM((columns, rows), F32),
@@ -430,6 +459,7 @@
             pltpu.VMEM((CHUNKS, piece, lanes), BF16),
             pltpu.VMEM((CHUNKS, row_count, piece, lanes), BF16),
             dma((5,)),
+            dma((3,)),
             dma((sub_count,)),
             dma((sub_count,)),
             dma((CHUNKS, sub_count)),
@@ -442,7 +472,7 @@
             dma((CHUNKS, row_count)),
         ],
         compiler_params=pltpu.CompilerParams(
-            collective_id=0, has_side_effects=True, vmem_limit_bytes=54700 * 1024
+            collective_id=0, has_side_effects=True, vmem_limit_bytes=61 * 1024 * 1024
         ),
         name="soft_pq_backward",
     )(
@@ -452,18 +482,8 @@
         centroid_tables.reshape(subs * width, codes),
         softness_factor,
     )
-    if share:
-        results = pl.pallas_call(
-            store_kernel,
-            out_shape=tuple(jax.ShapeDtypeStruct(r.shape, r.dtype) for r in results),
-            in_specs=[vmem, vmem, vmem],
-            out_specs=(hbm, hbm, hbm),
-            scratch_shapes=[dma((3,))],
-            name="store_results",
-        )(*results)
-        input_grad, rotation_grad, code_grad = results
-    else:
-        input_grad, rotation_grad, code_grad = results
+    input_grad, rotation_grad, code_grad = results
+    if not share:
         rotation_grad = lax.psum_scatter(rotation_grad.T, "row", scatter_dimension=0, tiled=True)
         code_grad = lax.psum(code_grad, "row")
     return input_grad, rotation_grad, code_grad.reshape(subs, width, codes)

time: 36.7 us -> 36.5 us (level)
  Pallas kernels: 33.2 us -> 32.7 us
    pallas_call x1 -> x0, Pallas kernels: 1.9 us -> none  [on_device(): pl.pallas_call(store_kernel, out_shape=tuple((jax.ShapeDtypeStruct(r.shap...]
    pallas_call x1, Pallas kernels: 31.3 us -> 32.7 us  [on_device(): pl.pallas_call(functools.partial(kernel, row_count, sub_count, share), ou...]
    unnamed x8 -> x7, local copies, waits for them, and re-layouts: 2.63 us -> 2.98 us
where the time goes in v2:
time: 36.5 us; the launch traced here: 36.4 us
  Pallas kernels  32.7 us (90%)
  local copies, waits for them, and re-layouts  2.98 us (8%)
  between operations  0.66 us (2%)
    pallas_call x1, Pallas kernels, on_device(): pl.pallas_call(functools.partial(kernel, row_count, sub_count, share), ou...  32.7 us
    unnamed x7, local copies, waits for them, and re-layouts  2.98 us

profile of v2, /device:TPU:0, one launch (start us, length us, event | category | flops | bytes accessed | tf_op | source)
XLA Modules:
  0.0 36.4 jit_solution(12220197339650603801)
XLA Ops:
  0.6 32.7 %soft_pq_backward.1 = (bf16[256,256]{1,0:T(8,128)(2,1)}, f32[128,256]{1,0:T(8,128)}, f32[256,256]{1,0:T(8,128)}) custom-call(bf16[256,1024]{1,0:T(8,128)(2,1)} %x_hbm.1, bf16[256,1024]{1,0:T(8,128)(2,1)} %u_hbm.1, bf16[1024,256]{1,0:T(8,128)(2,1)} %w_hbm.1, f32[256,256]{1,0:T(8,128)} %bitcast.3, f32[32]{0:T(128)} %temper_hbm.1), custom_call_target="tpu_custom_call" | custom-call | tf_op jit(solution)/shard_map/soft_pq_backward/pallas_call | solution.py:429
  33.4 0.0 copy-start.1
  33.4 0.0 copy-start
  33.4 1.6 %copy.11 = bf16[256,256]{1,0:T(8,128)(2,1)} copy(bf16[256,256]{1,0:T(8,128)(2,1)} %get-tuple-element.12) | data formatting | bytes 262144
  35.0 0.0 copy-done.1
  35.0 0.7 %copy.12 = f32[128,256]{1,0:T(8,128)} copy(f32[128,256]{1,0:T(8,128)S(1)} %copy-done.1) | data formatting | bytes 262144
  35.7 0.0 copy-done
  35.7 0.7 %copy.13 = f32[32,8,256]{2,1,0:T(8,128)} copy(f32[32,8,256]{2,1,0:T(8,128)S(1)} %bitcast.2) | data formatting | bytes 524288
Async XLA Ops:
  33.4 1.6 %copy-start.1 = (f32[128,256]{1,0:T(8,128)S(1)}, f32[128,256]{1,0:T(8,128)}, u32[]{:S(2)}) copy-start(f32[128,256]{1,0:T(8,128)} %get-tuple-element.13) | copy-start | bytes 393220
  33.4 2.3 %copy-start = (f32[256,256]{1,0:T(8,128)S(1)}, f32[256,256]{1,0:T(8,128)}, u32[]{:S(2)}) copy-start(f32[256,256]{1,0:T(8,128)} %get-tuple-element.8) | copy-start | bytes 786436

commit v3 on v2

--- a/solution.py
+++ b/solution.py
@@ -94,12 +94,10 @@
         left = jnp.concatenate(lefts[j] + lefts[j + 1], 0).astype(BF16).T
         both.append(nn(left, rights[j]))
         both.append(nn(left, rights[j + 1]))
-    exps, exps_low = [], []
+    exps_low = []
     for j in range(GROUP):
         s = both[j][:, :rows]
-        e = jnp.exp2(s - jnp.max(s, 0, keepdims=True))
-        exps.append(e)
-        exps_low.append(e.astype(BF16))
+        exps_low.append(jnp.exp2(s - jnp.max(s, 0, keepdims=True)).astype(BF16))
     sums = [nn(books[j], exps_low[j]) for j in range(GROUP)]
     slopes, scales, to_assign, to_weight = [], [], [], []
     for j in range(GROUP):
@@ -108,7 +106,7 @@
         recon = (sums[j][0:8] + sums[j][8:16]) * back
         recon_ref[at[j], :] = recon
         mean = jnp.sum(g * recon, 0, keepdims=True)
-        slopes.append((exps[j] * (both[j][:, rows:] - mean)).astype(BF16))
+        slopes.append(exps_low[j] * (both[j][:, rows:] - mean).astype(BF16))
         scale = back * (2.0 / jnp.full((1, rows), temper_ref[first + j], F32))
         scales.append(scale)
         a1, a2 = split2(g * back)
@@ -199,6 +197,7 @@
     block = features // row_count
     half = codes // 2
     piece = span // rests if share else 16
+    sibling = sub + 1 - 2 * lax.rem(sub, 2)
 
     loads = [
         pltpu.make_async_copy(src, dst, load_sems.at[i])
@@ -247,18 +246,33 @@
     def w_copy(peer, slot):
         at = pl.ds(pl.multiple_of(peer * slab, slab), slab)
         return remote(
-            w_ref.at[at], w_all.at[slot], w_send.at[peer], w_recv.at[slot], (row, peer)
-        )
-
-    def g_copy(h, peer, slot):
+            w_hbm.at[at], w_all.at[slot], w_send.at[peer], w_recv.at[slot], (row, peer)
+        )
+
+    def g_copy(h, way, peer, slot):
         at = pl.ds(pl.multiple_of(h * span, span), span)
         return remote(
             g_all.at[slot, at],
             g_all.at[slot, at],
-            g_send.at[h, peer],
+            g_send.at[h, way],
             g_recv.at[h, slot],
             (row, peer),
         )
+
+    def far_sends(h):
+        return [
+            g_copy(h, step - 1, lax.rem(sub + 2 * step, sub_count), sub)
+            for step in range(1, sub_count // 2)
+        ]
+
+    def near_send(h):
+        return g_copy(h, sub_count - 1, sibling, sub)
+
+    def forwards(h):
+        return [
+            g_copy(h, sub_count // 2 + step - 1, sibling, lax.rem(sub + 2 * step, sub_count))
+            for step in range(1, sub_count // 2)
+        ]
 
     def pair_copy(h):
         return remote(
@@ -294,10 +308,20 @@
 
         lax.fori_loop(0, per // GROUP, body, 0)
 
-    def send_grad(h):
+    def store_grad(h):
         at = pl.ds(pl.multiple_of(h * span, span), span)
         g_all[sub, at, :] = grad[at, :].astype(BF16)
-        for_peers(sub, sub_count, lambda peer: g_copy(h, peer, sub).start())
+
+    def send_grad(h):
+        for copy in far_sends(h):
+            copy.start()
+        near_send(h).start()
+
+    def forward_grad(h):
+        for step in range(1, sub_count // 2):
+            g_copy(h, 0, sub, lax.rem(sub + 2 * step, sub_count)).wait_recv()
+        for copy in forwards(h):
+            copy.start()
 
     def send_pair(h):
         at = pl.ds(pl.multiple_of(h * span, span), span)
@@ -351,6 +375,11 @@
                     other % 2 * half : (other % 2 + 1) * half,
                 ] = code_all[h, other].astype(F32)
 
+    pl.semaphore_wait(barrier, sub_count - 1 + (row_count - 1 if share else 0))
+    for step in range(1, sub_count // 2):
+        for side in (sub, sibling):
+            w_copy(lax.rem(side + 2 * step, sub_count), sub).start()
+    w_copy(sibling, sub).start()
     loads[0].wait()
     loads[1].wait()
     turned[...] = nn(x_ref[...], w_ref[...]).T
@@ -358,29 +387,32 @@
     slope[...] = nn(u_ref[...], w_ref[...]).T
     loads[3].wait()
     loads[4].wait()
-    pl.semaphore_wait(barrier, sub_count - 1 + (row_count - 1 if share else 0))
-    for_peers(sub, sub_count, lambda peer: w_copy(peer, sub).start())
 
     def chunk(h, carry):
         work(h)
+        store_grad(h)
+        send_pair(h)
         send_grad(h)
-        send_pair(h)
         pl.when(h >= 1)(lambda: send_rest(h - 1))
+        pl.when(h >= 1)(lambda: forward_grad(h - 1))
         pl.when(h >= 2)(lambda: finish_rest(h - 2))
         return carry
 
     lax.fori_loop(0, CHUNKS, chunk, 0)
+    forward_grad(CHUNKS - 1)
     send_rest(CHUNKS - 1)
     finish_rest(CHUNKS - 2)
 
     for_peers(sub, sub_count, lambda peer: w_copy(sub, peer).wait_recv())
     w_all[sub] = w_ref[pl.ds(pl.multiple_of(sub * slab, slab), slab), :]
     for h in range(CHUNKS):
-        for_peers(sub, sub_count, lambda peer: g_copy(h, sub, peer).wait_recv())
+        g_copy(h, 0, sub, sibling).wait_recv()
+        for step in range(1, sub_count // 2):
+            g_copy(h, 0, sub, lax.rem(sibling + 2 * step, sub_count)).wait_recv()
     total = nn(w_all[0], g_all[0]).astype(BF16).astype(F32)
     for other in range(1, sub_count):
         total += nn(w_all[other], g_all[other]).astype(BF16).astype(F32)
-    input_ref[...] = total.T.astype(BF16)
+    input_ref[...] = low(total.T)
     stores[0].start()
 
     finish_rest(CHUNKS - 1)
@@ -393,7 +425,8 @@
 
     for_peers(sub, sub_count, lambda peer: w_copy(peer, sub).wait_send())
     for h in range(CHUNKS):
-        for_peers(sub, sub_count, lambda peer: g_copy(h, peer, sub).wait_send())
+        for copy in far_sends(h) + [near_send(h)] + forwards(h):
+            copy.wait_send()
         if share:
             pair_copy(h).wait_send()
             for_peers(rest, rests, lambda peer: rest_copy(h, peer, rest).wait_send())
@@ -429,7 +462,7 @@
     results = pl.pallas_call(
         functools.partial(kernel, row_count, sub_count, share),
         out_shape=(
-            jax.ShapeDtypeStruct((rows, slab), BF16),
+            jax.ShapeDtypeStruct((rows, slab), F32),
             jax.ShapeDtypeStruct(rotation_shape, F32),
             jax.ShapeDtypeStruct((subs * width, codes), F32),
         ),
@@ -441,7 +474,7 @@
             pltpu.VMEM((features, columns), BF16),
             pltpu.VMEM((columns, codes), F32),
             pltpu.SMEM((subs,), F32),
-            pltpu.VMEM((rows, slab), BF16),
+            pltpu.VMEM((rows, slab), F32),
             pltpu.VMEM(rotation_shape, F32),
             pltpu.VMEM((subs * width, codes), F32),
             pltpu.VMEM((columns, rows), F32),
@@ -486,7 +519,7 @@
     if not share:
         rotation_grad = lax.psum_scatter(rotation_grad.T, "row", scatter_dimension=0, tiled=True)
         code_grad = lax.psum(code_grad, "row")
-    return input_grad, rotation_grad, code_grad.reshape(subs, width, codes)
+    return input_grad.astype(BF16), rotation_grad, code_grad.reshape(subs, width, codes)
 
 
 def solution(mesh):

time: 36.5 us -> 38 us (1.041)
  other arithmetic: 0 us -> 1.67 us
  local copies, waits for them, and re-layouts: 2.98 us -> 1.37 us
  Pallas kernels: 32.7 us -> 34.1 us
    convert_element_type x0 -> x1, other arithmetic: none -> 1.67 us  [on_device(): input_grad.astype(BF16)]
    unnamed x7 -> x6, local copies, waits for them, and re-layouts: 2.98 us -> 1.37 us
    pallas_call x1, Pallas kernels: 32.7 us -> 34.1 us  [on_device(): pl.pallas_call(functools.partial(kernel, row_count, sub_count, share), ou...]
where the time goes in v3:
time: 38 us; the launch traced here: 37.8 us
  Pallas kernels  34.1 us (90%)
  other arithmetic  1.67 us (4%)
  local copies, waits for them, and re-layouts  1.37 us (4%)
  between operations  0.66 us (2%)
    pallas_call x1, Pallas kernels, on_device(): pl.pallas_call(functools.partial(kernel, row_count, sub_count, share), ou...  34.1 us
    convert_element_type x1, other arithmetic, on_device(): input_grad.astype(BF16)  1.67 us
    unnamed x6, local copies, waits for them, and re-layouts  1.37 us

profile of v3, /device:TPU:0, one launch (start us, length us, event | category | flops | bytes accessed | tf_op | source)
XLA Modules:
  0.0 37.8 jit_solution(1768804608301149305)
XLA Ops:
  0.6 34.1 %soft_pq_backward.1 = (f32[256,256]{1,0:T(8,128)}, f32[128,256]{1,0:T(8,128)}, f32[256,256]{1,0:T(8,128)}) custom-call(bf16[256,1024]{1,0:T(8,128)(2,1)} %x_hbm.1, bf16[256,1024]{1,0:T(8,128)(2,1)} %u_hbm.1, bf16[1024,256]{1,0:T(8,128)(2,1)} %w_hbm.1, f32[256,256]{1,0:T(8,128)} %bitcast.3, f32[32]{0:T(128)} %temper_hbm.1), custom_call_target="tpu_custom_call" | custom-call | tf_op jit(solution)/shard_map/soft_pq_backward/pallas_call | solution.py:462
  34.8 0.0 copy-start.1
  34.8 0.0 copy-start
  34.8 1.7 %convert_element_type.3 = bf16[256,256]{1,0:T(8,128)(2,1)} convert(f32[256,256]{1,0:T(8,128)} %get-tuple-element.6) | non-fusion elementwise | flops 65536 | bytes 393216 | tf_op jit(solution)/shard_map/convert_element_type | solution.py:522
  36.5 0.0 copy-done.1
  36.5 0.7 %copy.10 = f32[128,256]{1,0:T(8,128)} copy(f32[128,256]{1,0:T(8,128)S(1)} %copy-done.1) | data formatting | bytes 262144
  37.1 0.0 copy-done
  37.1 0.7 %copy.11 = f32[32,8,256]{2,1,0:T(8,128)} copy(f32[32,8,256]{2,1,0:T(8,128)S(1)} %bitcast.2) | data formatting | bytes 524288
Async XLA Ops:
  34.8 1.7 %copy-start.1 = (f32[128,256]{1,0:T(8,128)S(1)}, f32[128,256]{1,0:T(8,128)}, u32[]{:S(2)}) copy-start(f32[128,256]{1,0:T(8,128)} %get-tuple-element.13) | copy-start | bytes 393220
  34.8 2.3 %copy-start = (f32[256,256]{1,0:T(8,128)S(1)}, f32[256,256]{1,0:T(8,128)}, u32[]{:S(2)}) copy-start(f32[256,256]{1,0:T(8,128)} %get-tuple-element.8) | copy-start | bytes 786436

commit v4 on v3

--- a/solution.py
+++ b/solution.py
@@ -94,10 +94,12 @@
         left = jnp.concatenate(lefts[j] + lefts[j + 1], 0).astype(BF16).T
         both.append(nn(left, rights[j]))
         both.append(nn(left, rights[j + 1]))
-    exps_low = []
+    exps, exps_low = [], []
     for j in range(GROUP):
         s = both[j][:, :rows]
-        exps_low.append(jnp.exp2(s - jnp.max(s, 0, keepdims=True)).astype(BF16))
+        e = jnp.exp2(s - jnp.max(s, 0, keepdims=True))
+        exps.append(e)
+        exps_low.append(e.astype(BF16))
     sums = [nn(books[j], exps_low[j]) for j in range(GROUP)]
     slopes, scales, to_assign, to_weight = [], [], [], []
     for j in range(GROUP):
@@ -106,7 +108,7 @@
         recon = (sums[j][0:8] + sums[j][8:16]) * back
         recon_ref[at[j], :] = recon
         mean = jnp.sum(g * recon, 0, keepdims=True)
-        slopes.append(exps_low[j] * (both[j][:, rows:] - mean).astype(BF16))
+        slopes.append((exps[j] * (both[j][:, rows:] - mean)).astype(BF16))
         scale = back * (2.0 / jnp.full((1, rows), temper_ref[first + j], F32))
         scales.append(scale)
         a1, a2 = split2(g * back)
@@ -170,6 +172,10 @@
     pair_got,
     rest_out,
     rest_got,
+    cross_out,
+    cross_got,
+    swap_out,
+    swap_got,
     code_sum,
     code_all,
     load_sems,
@@ -182,6 +188,10 @@
     pair_recv,
     rest_send,
     rest_recv,
+    cross_send,
+    cross_recv,
+    swap_send,
+    swap_recv,
     code_send,
     code_recv,
 ):
@@ -196,6 +206,7 @@
     partner = rest * 2 + (1 - bit)
     block = features // row_count
     half = codes // 2
+    mid = span // 2
     piece = span // rests if share else 16
     sibling = sub + 1 - 2 * lax.rem(sub, 2)
 
@@ -288,6 +299,20 @@
             (peer * 2 + bit, sub),
         )
 
+    def cross_copy(h, peer, slot):
+        return remote(
+            cross_out.at[h, peer],
+            cross_got.at[h, slot],
+            cross_send.at[h, peer],
+            cross_recv.at[h, slot],
+            (peer * 2 + bit, sub),
+        )
+
+    def swap_copy(h):
+        return remote(
+            swap_out.at[h, 1 - bit], swap_got.at[h], swap_send.at[h], swap_recv.at[h], (partner, sub)
+        )
+
     def code_copy(h, peer, slot):
         return remote(
             code_sum.at[h],
@@ -328,12 +353,17 @@
         local = nn(g_all[sub, at, :], x_ref[...]) + nn(recon[at, :].astype(BF16), u_ref[...])
         if share:
             for peer in range(rests):
+                codes_at = pl.ds(pl.multiple_of(h * span + peer * piece, piece), piece)
                 for side in range(2):
                     start = (peer * 2 + side) * block
-                    pair_out[h, side, peer] = local[:, start : start + block].astype(BF16)
-            for side in range(2):
-                pair_out[h, side, rests] = cg[at, side * half : (side + 1) * half].astype(BF16)
+                    part = local[:, start : start + block].astype(BF16)
+                    pair_out[h, side, peer] = part[:mid]
+                    cross_out[h, peer, side, :mid, :] = part[mid:]
+                    cross_out[h, peer, side, mid:, :] = cg[
+                        codes_at, side * half : (side + 1) * half
+                    ].astype(BF16)
             pair_copy(h).start()
+            for_peers(rest, rests, lambda peer: cross_copy(h, peer, rest).start())
         else:
             rotation_ref[at, :] = local
             codes_ref[at, :] = cg[at, :]
@@ -342,28 +372,31 @@
         if share:
             pair_copy(h).wait_recv()
             for peer in range(rests):
-                rest_out[h, peer, :span, :] = (
+                rest_out[h, peer] = (
                     pair_out[h, bit, peer].astype(F32) + pair_got[h, peer].astype(F32)
                 ).astype(BF16)
-                at = pl.ds(peer * piece, piece)
-                rest_out[h, peer, span:, :] = (
-                    pair_out[h, bit, rests, at].astype(F32) + pair_got[h, rests, at].astype(F32)
-                ).astype(BF16)
             for_peers(rest, rests, lambda peer: rest_copy(h, peer, rest).start())
+            for_peers(rest, rests, lambda peer: cross_copy(h, rest, peer).wait_recv())
+            cross_got[h, rest] = cross_out[h, rest]
+            total = cross_got[h, 0].astype(F32)
+            for other in range(1, rests):
+                total += cross_got[h, other].astype(F32)
+            swap_out[h] = total.astype(BF16)
+            swap_copy(h).start()
 
     def finish_rest(h):
         if share:
+            swap_copy(h).wait_recv()
+            total = swap_out[h, bit].astype(F32) + swap_got[h].astype(F32)
+            code_sum[h] = total[mid:].astype(BF16)
+            for_peers(row, row_count, lambda peer: code_copy(h, peer, row).start())
+            rot_sum[pl.ds(pl.multiple_of(h * span + mid, mid), mid), :] = total[:mid]
             for_peers(rest, rests, lambda peer: rest_copy(h, rest, peer).wait_recv())
             rest_got[h, rest] = rest_out[h, rest]
-            total = rest_got[h, 0, span:, :].astype(F32)
+            total = rest_got[h, 0].astype(F32)
             for other in range(1, rests):
-                total += rest_got[h, other, span:, :].astype(F32)
-            code_sum[h] = total.astype(BF16)
-            for_peers(row, row_count, lambda peer: code_copy(h, peer, row).start())
-            total = rest_got[h, 0, :span, :].astype(F32)
-            for other in range(1, rests):
-                total += rest_got[h, other, :span, :].astype(F32)
-            rot_sum[pl.ds(pl.multiple_of(h * span, span), span), :] = total
+                total += rest_got[h, other].astype(F32)
+            rot_sum[pl.ds(pl.multiple_of(h * span, mid), mid), :] = total
 
     def finish_codes(h):
         if share:
@@ -430,6 +463,8 @@
         if share:
             pair_copy(h).wait_send()
             for_peers(rest, rests, lambda peer: rest_copy(h, peer, rest).wait_send())
+            for_peers(rest, rests, lambda peer: cross_copy(h, peer, rest).wait_send())
+            swap_copy(h).wait_send()
             for_peers(row, row_count, lambda peer: code_copy(h, peer, row).wait_send())
     for store in stores:
         store.wait()
@@ -455,6 +490,7 @@
     )
     pieces = rests if share else 1
     piece = span // pieces
+    mid = span // 2
     lanes = block if share else 128
     dma = pltpu.SemaphoreType.DMA
     hbm = pl.BlockSpec(memory_space=pltpu.HBM)
@@ -485,10 +521,14 @@
             pltpu.VMEM((sub_count, slab, columns), BF16),
             pltpu.VMEM((sub_count, columns, rows), BF16),
             pltpu.VMEM((columns, lanes), F32),
-            pltpu.VMEM((CHUNKS, 2, pieces + 1, span, lanes), BF16),
-            pltpu.VMEM((CHUNKS, pieces + 1, span, lanes), BF16),
-            pltpu.VMEM((CHUNKS, pieces, span + piece, lanes), BF16),
-            pltpu.VMEM((CHUNKS, pieces, span + piece, lanes), BF16),
+            pltpu.VMEM((CHUNKS, 2, pieces, mid, lanes), BF16),
+            pltpu.VMEM((CHUNKS, pieces, mid, lanes), BF16),
+            pltpu.VMEM((CHUNKS, pieces, mid, lanes), BF16),
+            pltpu.VMEM((CHUNKS, pieces, mid, lanes), BF16),
+            pltpu.VMEM((CHUNKS, pieces, 2, mid + piece, lanes), BF16),
+            pltpu.VMEM((CHUNKS, pieces, 2, mid + piece, lanes), BF16),
+            pltpu.VMEM((CHUNKS, 2, mid + piece, lanes), BF16),
+            pltpu.VMEM((CHUNKS, mid + piece, lanes), BF16),
             pltpu.VMEM((CHUNKS, piece, lanes), BF16),
             pltpu.VMEM((CHUNKS, row_count, piece, lanes), BF16),
             dma((5,)),
@@ -501,6 +541,10 @@
             dma((CHUNKS,)),
             dma((CHUNKS, pieces)),
             dma((CHUNKS, pieces)),
+            dma((CHUNKS, pieces)),
+            dma((CHUNKS, pieces)),
+            dma((CHUNKS,)),
+            dma((CHUNKS,)),
             dma((CHUNKS, row_count)),
             dma((CHUNKS, row_count)),
         ],

time: 38 us -> 38.4 us (1.011)
  Pallas kernels: 34.1 us -> 34.5 us
where the time goes in v4:
time: 38.4 us; the launch traced here: 38.2 us
  Pallas kernels  34.5 us (90%)
  other arithmetic  1.67 us (4%)
  local copies, waits for them, and re-layouts  1.37 us (4%)
  between operations  0.66 us (2%)
    pallas_call x1, Pallas kernels, on_device(): pl.pallas_call(functools.partial(kernel, row_count, sub_count, share), ou...  34.5 us
    convert_element_type x1, other arithmetic, on_device(): input_grad.astype(BF16)  1.67 us
    unnamed x6, local copies, waits for them, and re-layouts  1.37 us

profile of v4, /device:TPU:0, one launch (start us, length us, event | category | flops | bytes accessed | tf_op | source)
XLA Modules:
  0.0 38.2 jit_solution(1103197480709380941)
XLA Ops:
  0.6 34.5 %soft_pq_backward.1 = (f32[256,256]{1,0:T(8,128)}, f32[128,256]{1,0:T(8,128)}, f32[256,256]{1,0:T(8,128)}) custom-call(bf16[256,1024]{1,0:T(8,128)(2,1)} %x_hbm.1, bf16[256,1024]{1,0:T(8,128)(2,1)} %u_hbm.1, bf16[1024,256]{1,0:T(8,128)(2,1)} %w_hbm.1, f32[256,256]{1,0:T(8,128)} %bitcast.3, f32[32]{0:T(128)} %temper_hbm.1), custom_call_target="tpu_custom_call" | custom-call | tf_op jit(solution)/shard_map/soft_pq_backward/pallas_call | solution.py:498
  35.2 0.0 copy-start.1
  35.2 0.0 copy-start
  35.2 1.7 %convert_element_type.3 = bf16[256,256]{1,0:T(8,128)(2,1)} convert(f32[256,256]{1,0:T(8,128)} %get-tuple-element.6) | non-fusion elementwise | flops 65536 | bytes 393216 | tf_op jit(solution)/shard_map/convert_element_type | solution.py:566
  36.8 0.0 copy-done.1
  36.8 0.7 %copy.10 = f32[128,256]{1,0:T(8,128)} copy(f32[128,256]{1,0:T(8,128)S(1)} %copy-done.1) | data formatting | bytes 262144
  37.5 0.0 copy-done
  37.5 0.7 %copy.11 = f32[32,8,256]{2,1,0:T(8,128)} copy(f32[32,8,256]{2,1,0:T(8,128)S(1)} %bitcast.2) | data formatting | bytes 524288
Async XLA Ops:
  35.2 1.7 %copy-start.1 = (f32[128,256]{1,0:T(8,128)S(1)}, f32[128,256]{1,0:T(8,128)}, u32[]{:S(2)}) copy-start(f32[128,256]{1,0:T(8,128)} %get-tuple-element.13) | copy-start | bytes 393220
  35.2 2.3 %copy-start = (f32[256,256]{1,0:T(8,128)S(1)}, f32[256,256]{1,0:T(8,128)}, u32[]{:S(2)}) copy-start(f32[256,256]{1,0:T(8,128)} %get-tuple-element.8) | copy-start | bytes 786436

commit v5 on v1

--- a/solution.py
+++ b/solution.py
@@ -128,14 +128,17 @@
     w_hbm,
     book_hbm,
     temper_hbm,
-    input_ref,
-    rotation_ref,
-    codes_ref,
+    input_hbm,
+    rotation_hbm,
+    codes_hbm,
     x_ref,
     u_ref,
     w_ref,
     book_ref,
     temper_ref,
+    input_ref,
+    rotation_ref,
+    codes_ref,
     turned,
     slope,
     grad,
@@ -148,9 +151,11 @@
     pair_got,
     rest_out,
     rest_got,
+    direct_got,
     code_sum,
     code_all,
     load_sems,
+    store_sems,
     w_send,
     w_recv,
     g_send,
@@ -159,6 +164,8 @@
     pair_recv,
     rest_send,
     rest_recv,
+    direct_send,
+    direct_recv,
     code_send,
     code_recv,
 ):
@@ -173,6 +180,7 @@
     partner = rest * 2 + (1 - bit)
     block = features // row_count
     half = codes // 2
+    last = CHUNKS - 1
     piece = span // rests if share else 16
 
     loads = [
@@ -190,6 +198,13 @@
     for load in loads:
         load.start()
 
+    stores = [
+        pltpu.make_async_copy(src, dst, store_sems.at[i])
+        for i, (src, dst) in enumerate(
+            [(input_ref, input_hbm), (rotation_ref, rotation_hbm), (codes_ref, codes_hbm)]
+        )
+    ]
+
     barrier = pltpu.get_barrier_semaphore()
 
     def greet_row(peer):
@@ -242,6 +257,15 @@
             (peer * 2 + bit, sub),
         )
 
+    def direct_copy(h, peer, slot):
+        return remote(
+            pair_out.at[h, lax.rem(peer, 2), peer // 2],
+            direct_got.at[slot],
+            direct_send.at[peer],
+            direct_recv.at[slot],
+            (peer, sub),
+        )
+
     def code_copy(h, peer, slot):
         return remote(
             code_sum.at[h],
@@ -263,21 +287,24 @@
         lax.fori_loop(0, per // GROUP, body, 0)
 
     def send_grad(h):
+        for_peers(sub, sub_count, lambda peer: g_copy(h, peer, sub).start())
+
+    def send_pair(h):
         at = pl.ds(h * span, span)
         g_all[sub, at, :] = grad[at, :].astype(BF16)
-        for_peers(sub, sub_count, lambda peer: g_copy(h, peer, sub).start())
-
-    def send_pair(h):
-        at = pl.ds(h * span, span)
         local = nn(g_all[sub, at, :], x_ref[...]) + nn(recon[at, :].astype(BF16), u_ref[...])
         if share:
             for peer in range(rests):
                 for side in range(2):
                     start = (peer * 2 + side) * block
-                    pair_out[h, side, peer] = local[:, start : start + block].astype(BF16)
-            for side in range(2):
-                pair_out[h, side, rests] = cg[at, side * half : (side + 1) * half].astype(BF16)
-            pair_copy(h).start()
+                    pair_out[h, side, peer, :span, :] = local[:, start : start + block].astype(BF16)
+                    pair_out[h, side, peer, span:, :] = cg[
+                        pl.ds(h * span + peer * piece, piece), side * half : (side + 1) * half
+                    ].astype(BF16)
+            if h < last:
+                pair_copy(h).start()
+            else:
+                for_peers(row, row_count, lambda peer: direct_copy(h, peer, row).start())
         else:
             rotation_ref[at, :] = local
             codes_ref[at, :] = cg[at, :]
@@ -286,12 +313,8 @@
         if share:
             pair_copy(h).wait_recv()
             for peer in range(rests):
-                rest_out[h, peer, :span, :] = (
+                rest_out[h, peer] = (
                     pair_out[h, bit, peer].astype(F32) + pair_got[h, peer].astype(F32)
-                ).astype(BF16)
-                at = pl.ds(peer * piece, piece)
-                rest_out[h, peer, span:, :] = (
-                    pair_out[h, bit, rests, at].astype(F32) + pair_got[h, rests, at].astype(F32)
                 ).astype(BF16)
             for_peers(rest, rests, lambda peer: rest_copy(h, peer, rest).start())
 
@@ -309,6 +332,20 @@
                 total += rest_got[h, other, :span, :].astype(F32)
             rot_sum[pl.ds(h * span, span), :] = total
 
+    def finish_direct(h):
+        if share:
+            for_peers(row, row_count, lambda peer: direct_copy(h, row, peer).wait_recv())
+            direct_got[row] = pair_out[h, bit, rest]
+            total = direct_got[0, span:, :].astype(F32)
+            for other in range(1, row_count):
+                total += direct_got[other, span:, :].astype(F32)
+            code_sum[h] = total.astype(BF16)
+            for_peers(row, row_count, lambda peer: code_copy(h, peer, row).start())
+            total = direct_got[0, :span, :].astype(F32)
+            for other in range(1, row_count):
+                total += direct_got[other, :span, :].astype(F32)
+            rot_sum[pl.ds(h * span, span), :] = total
+
     def finish_codes(h):
         if share:
             for_peers(row, row_count, lambda peer: code_copy(h, row, peer).wait_recv())
@@ -331,15 +368,15 @@
 
     for h in range(CHUNKS):
         work(h)
+        send_pair(h)
         send_grad(h)
-        send_pair(h)
         if h >= 1:
             send_rest(h - 1)
         if h >= 2:
             finish_rest(h - 2)
-    send_rest(CHUNKS - 1)
-    finish_rest(CHUNKS - 2)
-
+    finish_rest(last - 1)
+
+    finish_direct(last)
     for_peers(sub, sub_count, lambda peer: w_copy(sub, peer).wait_recv())
     w_all[sub] = w_ref[pl.ds(pl.multiple_of(sub * slab, slab), slab), :]
     for h in range(CHUNKS):
@@ -348,29 +385,25 @@
     for other in range(1, sub_count):
         total += nn(w_all[other], g_all[other]).astype(BF16).astype(F32)
     input_ref[...] = total.T.astype(BF16)
-
-    finish_rest(CHUNKS - 1)
+    stores[0].start()
+
     if share:
         rotation_ref[...] = rot_sum[...].T
+    stores[1].start()
     for h in range(CHUNKS):
         finish_codes(h)
+    stores[2].start()
 
     for_peers(sub, sub_count, lambda peer: w_copy(peer, sub).wait_send())
     for h in range(CHUNKS):
         for_peers(sub, sub_count, lambda peer: g_copy(h, peer, sub).wait_send())
         if share:
-            pair_copy(h).wait_send()
-            for_peers(rest, rests, lambda peer: rest_copy(h, peer, rest).wait_send())
+            if h < last:
+                pair_copy(h).wait_send()
+                for_peers(rest, rests, lambda peer: rest_copy(h, peer, rest).wait_send())
+            else:
+                for_peers(row, row_count, lambda peer: direct_copy(h, peer, row).wait_send())
             for_peers(row, row_count, lambda peer: code_copy(h, peer, row).wait_send())
-
-
-def store_kernel(a_ref, b_ref, c_ref, a_out, b_out, c_out, sems):
-    stores = [
-        pltpu.make_async_copy(src, dst, sems.at[i])
-        for i, (src, dst) in enumerate([(a_ref, a_out), (b_ref, b_out), (c_ref, c_out)])
-    ]
-    for store in stores:
-        store.start()
     for store in stores:
         store.wait()
 
@@ -397,7 +430,6 @@
     piece = span // pieces
     lanes = block if share else 128
     dma = pltpu.SemaphoreType.DMA
-    vmem = pl.BlockSpec(memory_space=pltpu.VMEM)
     hbm = pl.BlockSpec(memory_space=pltpu.HBM)
     rotation_shape = (block, columns) if share else (columns, features)
     results = pl.pallas_call(
@@ -408,13 +440,16 @@
             jax.ShapeDtypeStruct((subs * width, codes), F32),
         ),
         in_specs=[hbm, hbm, hbm, hbm, hbm],
-        out_specs=(vmem, vmem, vmem),
+        out_specs=(hbm, hbm, hbm),
         scratch_shapes=[
             pltpu.VMEM((rows, features), BF16),
             pltpu.VMEM((rows, features), BF16),
             pltpu.VMEM((features, columns), BF16),
             pltpu.VMEM((columns, codes), F32),
             pltpu.SMEM((subs,), F32),
+            pltpu.VMEM((rows, slab), BF16),
+            pltpu.VMEM(rotation_shape, F32),
+            pltpu.VMEM((subs * width, codes), F32),
             pltpu.VMEM((columns, rows), F32),
             pltpu.VMEM((columns, rows), F32),
             pltpu.VMEM((columns, rows), F32),
@@ -423,13 +458,15 @@
             pltpu.VMEM((sub_count, slab, columns), BF16),
             pltpu.VMEM((sub_count, columns, rows), BF16),
             pltpu.VMEM((columns, lanes), F32),
-            pltpu.VMEM((CHUNKS, 2, pieces + 1, span, lanes), BF16),
-            pltpu.VMEM((CHUNKS, pieces + 1, span, lanes), BF16),
+            pltpu.VMEM((CHUNKS, 2, pieces, span + piece, lanes), BF16),
             pltpu.VMEM((CHUNKS, pieces, span + piece, lanes), BF16),
             pltpu.VMEM((CHUNKS, pieces, span + piece, lanes), BF16),
+            pltpu.VMEM((CHUNKS, pieces, span + piece, lanes), BF16),
+            pltpu.VMEM((row_count, span + piece, lanes), BF16),
             pltpu.VMEM((CHUNKS, piece, lanes), BF16),
             pltpu.VMEM((CHUNKS, row_count, piece, lanes), BF16),
             dma((5,)),
+            dma((3,)),
             dma((sub_count,)),
             dma((sub_count,)),
             dma((CHUNKS, sub_count)),
@@ -438,11 +475,13 @@
             dma((CHUNKS,)),
             dma((CHUNKS, pieces)),
             dma((CHUNKS, pieces)),
+            dma((row_count,)),
+            dma((row_count,)),
             dma((CHUNKS, row_count)),
             dma((CHUNKS, row_count)),
         ],
         compiler_params=pltpu.CompilerParams(
-            collective_id=0, has_side_effects=True, vmem_limit_bytes=54700 * 1024
+            collective_id=0, has_side_effects=True, vmem_limit_bytes=61 * 1024 * 1024
         ),
         name="soft_pq_backward",
     )(
@@ -452,18 +491,8 @@
         centroid_tables.reshape(subs * width, codes),
         softness_factor,
     )
-    if share:
-        results = pl.pallas_call(
-            store_kernel,
-            out_shape=tuple(jax.ShapeDtypeStruct(r.shape, r.dtype) for r in results),
-            in_specs=[vmem, vmem, vmem],
-            out_specs=(hbm, hbm, hbm),
-            scratch_shapes=[dma((3,))],
-            name="store_results",
-        )(*results)
-        input_grad, rotation_grad, code_grad = results
-    else:
-        input_grad, rotation_grad, code_grad = results
+    input_grad, rotation_grad, code_grad = results
+    if not share:
         rotation_grad = lax.psum_scatter(rotation_grad.T, "row", scatter_dimension=0, tiled=True)
         code_grad = lax.psum(code_grad, "row")
     return input_grad, rotation_grad, code_grad.reshape(subs, width, codes)

time: 36.7 us -> 35.4 us (0.965)
  Pallas kernels: 33.2 us -> 31.6 us
    pallas_call x1 -> x0, Pallas kernels: 1.9 us -> none  [on_device(): pl.pallas_call(store_kernel, out_shape=tuple((jax.ShapeDtypeStruct(r.shap...]
    unnamed x8 -> x7, local copies, waits for them, and re-layouts: 2.63 us -> 2.98 us
where the time goes in v5:
time: 35.4 us; the launch traced here: 35.2 us
  Pallas kernels  31.6 us (89%)
  local copies, waits for them, and re-layouts  2.98 us (8%)
  between operations  0.66 us (2%)
    pallas_call x1, Pallas kernels, on_device(): pl.pallas_call(functools.partial(kernel, row_count, sub_count, share), ou...  31.6 us
    unnamed x7, local copies, waits for them, and re-layouts  2.98 us

profile of v5, /device:TPU:0, one launch (start us, length us, event | category | flops | bytes accessed | tf_op | source)
XLA Modules:
  0.0 35.2 jit_solution(861733729675427335)
XLA Ops:
  0.6 31.6 %soft_pq_backward.1 = (bf16[256,256]{1,0:T(8,128)(2,1)}, f32[128,256]{1,0:T(8,128)}, f32[256,256]{1,0:T(8,128)}) custom-call(bf16[256,1024]{1,0:T(8,128)(2,1)} %x_hbm.1, bf16[256,1024]{1,0:T(8,128)(2,1)} %u_hbm.1, bf16[1024,256]{1,0:T(8,128)(2,1)} %w_hbm.1, f32[256,256]{1,0:T(8,128)} %bitcast.3, f32[32]{0:T(128)} %temper_hbm.1), custom_call_target="tpu_custom_call" | custom-call | tf_op jit(solution)/shard_map/soft_pq_backward/pallas_call | solution.py:435
  32.2 0.0 copy-start.1
  32.2 0.0 copy-start
  32.2 1.6 %copy.11 = bf16[256,256]{1,0:T(8,128)(2,1)} copy(bf16[256,256]{1,0:T(8,128)(2,1)} %get-tuple-element.12) | data formatting | bytes 262144
  33.8 0.0 copy-done.1
  33.8 0.7 %copy.12 = f32[128,256]{1,0:T(8,128)} copy(f32[128,256]{1,0:T(8,128)S(1)} %copy-done.1) | data formatting | bytes 262144
  34.5 0.0 copy-done
  34.5 0.7 %copy.13 = f32[32,8,256]{2,1,0:T(8,128)} copy(f32[32,8,256]{2,1,0:T(8,128)S(1)} %bitcast.2) | data formatting | bytes 524288
Async XLA Ops:
  32.2 1.6 %copy-start.1 = (f32[128,256]{1,0:T(8,128)S(1)}, f32[128,256]{1,0:T(8,128)}, u32[]{:S(2)}) copy-start(f32[128,256]{1,0:T(8,128)} %get-tuple-element.13) | copy-start | bytes 393220
  32.2 2.3 %copy-start = (f32[256,256]{1,0:T(8,128)S(1)}, f32[256,256]{1,0:T(8,128)}, u32[]{:S(2)}) copy-start(f32[256,256]{1,0:T(8,128)} %get-tuple-element.8) | copy-start | bytes 786436

commit v6 on v5

--- a/solution.py
+++ b/solution.py
@@ -10,7 +10,7 @@
 MESH = pl.DeviceIdType.MESH
 LOG2E = 1.4426950408889634
 CHUNKS = 4
-GROUP = 4
+GROUP = 8
 F32 = jnp.float32
 BF16 = jnp.bfloat16
 

time: 35.4 us -> 34.7 us (0.980)
  Pallas kernels: 31.6 us -> 30.9 us
    pallas_call x1, Pallas kernels: 31.6 us -> 30.9 us  [on_device(): pl.pallas_call(functools.partial(kernel, row_count, sub_count, share), ou...]
where the time goes in v6:
time: 34.7 us; the launch traced here: 34.6 us
  Pallas kernels  30.9 us (89%)
  local copies, waits for them, and re-layouts  2.98 us (9%)
  between operations  0.66 us (2%)
    pallas_call x1, Pallas kernels, on_device(): pl.pallas_call(functools.partial(kernel, row_count, sub_count, share), ou...  30.9 us
    unnamed x7, local copies, waits for them, and re-layouts  2.98 us

profile of v6, /device:TPU:0, one launch (start us, length us, event | category | flops | bytes accessed | tf_op | source)
XLA Modules:
  0.0 34.6 jit_solution(5639319627276483406)
XLA Ops:
  0.6 30.9 %soft_pq_backward.1 = (bf16[256,256]{1,0:T(8,128)(2,1)}, f32[128,256]{1,0:T(8,128)}, f32[256,256]{1,0:T(8,128)}) custom-call(bf16[256,1024]{1,0:T(8,128)(2,1)} %x_hbm.1, bf16[256,1024]{1,0:T(8,128)(2,1)} %u_hbm.1, bf16[1024,256]{1,0:T(8,128)(2,1)} %w_hbm.1, f32[256,256]{1,0:T(8,128)} %bitcast.3, f32[32]{0:T(128)} %temper_hbm.1), custom_call_target="tpu_custom_call" | custom-call | tf_op jit(solution)/shard_map/soft_pq_backward/pallas_call | solution.py:435
  31.6 0.0 copy-start.1
  31.6 0.0 copy-start
  31.6 1.6 %copy.11 = bf16[256,256]{1,0:T(8,128)(2,1)} copy(bf16[256,256]{1,0:T(8,128)(2,1)} %get-tuple-element.12) | data formatting | bytes 262144
  33.2 0.0 copy-done.1
  33.2 0.7 %copy.12 = f32[128,256]{1,0:T(8,128)} copy(f32[128,256]{1,0:T(8,128)S(1)} %copy-done.1) | data formatting | bytes 262144
  33.9 0.0 copy-done
  33.9 0.7 %copy.13 = f32[32,8,256]{2,1,0:T(8,128)} copy(f32[32,8,256]{2,1,0:T(8,128)S(1)} %bitcast.2) | data formatting | bytes 524288
Async XLA Ops:
  31.6 1.6 %copy-start.1 = (f32[128,256]{1,0:T(8,128)S(1)}, f32[128,256]{1,0:T(8,128)}, u32[]{:S(2)}) copy-start(f32[128,256]{1,0:T(8,128)} %get-tuple-element.13) | copy-start | bytes 393220
  31.6 2.3 %copy-start = (f32[256,256]{1,0:T(8,128)S(1)}, f32[256,256]{1,0:T(8,128)}, u32[]{:S(2)}) copy-start(f32[256,256]{1,0:T(8,128)} %get-tuple-element.8) | copy-start | bytes 786436
